TPU v7x, 256 devices: a whole 4x4x8 slice. The times are simulated.
256 devices in a mesh: dp: 16 (over z, x_lo), cont: 16 (over y, x_hi, core).
Axes of the slice: x: 4 (x_hi: 2, x_lo: 2; x = x_hi * 2 + x_lo), y: 4, z: 8, core: 2. Of those that a mesh axis runs over, the one named last changes fastest.
Arguments:
- tokens: bfloat16 [32768, 8192], P(('dp', 'cont')), may hold values from -6 to 6
- frozen_step_queries: bfloat16 [32768, 8192], P(('dp', 'cont')), may hold values from -96 to 96
- step_token_keys: bfloat16 [32768, 1024], P(('dp', 'cont')), may hold values from -6 to 6
- step_token_values: bfloat16 [32768, 1024], P(('dp', 'cont')), may hold values from -6 to 6
- prefix_key_table: bfloat16 [8192, 1024], P(('dp', 'cont')), may hold values from -4 to 4
- prefix_value_table: bfloat16 [8192, 1024], P(('dp', 'cont')), may hold values from -6 to 6
- adapter_down_map: bfloat16 [16, 8192], replicated, may hold values from -0.0625 to 0.0625
- adapter_up_map: bfloat16 [16, 8192], replicated, may hold values from -1.5 to 1.5
- readout: bfloat16 [8192], replicated, may hold values from -0.0625 to 0.0625
- step_pair_lengths: int32 [256, 2], P(('dp', 'cont')), may hold values from 32 to 64, as said below
- prefix_length_table: int32 [16], P('dp'), may hold values from 32 to 512, as said below
- prefix_block_mask: int32 [512, 16], P(('dp', 'cont')), may hold values from 0 to 1, as said below
Outputs:
- loss_total: float32 [], replicated
- grad_down: float32 [16, 8192], replicated
- up_map_gradient: float32 [16, 8192], replicated
Inputs may be any that keep to these rules, and one draw needn't show every extreme that they name: `step_pair_lengths`: each length is at least 32, and some step has exactly 64. `prefix_length_table`: a multiple of 32; some group's prefix fills all 512 slots. `prefix_block_mask`: the first block is always 1.
All inputs are finite; a program needn't handle non-finite values.
Results may differ from a plain program's by a relative error of at most 0.025.
Values may be sent and summed in bfloat16 or wider, within the bound.
A program may use at most 128 MiB of HBM per device.

v0:
```python
import jax
import jax.numpy as jnp
from jax import lax
from jax.sharding import PartitionSpec as P

HQ = 64
KVH = 8
HD = 128
BLOCK = 32
QUERY_FEATURES = 8192


NEG = -1e30
BETA = 0.1
ADAPTER_SCALE = 2.0
LOSS_SCALE = 1024.0


def local(
    tokens,
    frozen_step_queries,
    step_token_keys,
    step_token_values,
    prefix_key_table,
    prefix_value_table,
    adapter_down_map,
    adapter_up_map,
    readout,
    step_pair_lengths,
    prefix_length_table,
    prefix_block_mask,
):
    rows_all = tokens.shape[0]
    half = rows_all // 2
    groups = HQ // KVH
    factor = HD ** (-0.5)
    down_projection = jnp.dot(
        tokens, adapter_down_map.T, preferred_element_type=jnp.float32
    ).astype(jnp.bfloat16)
    adapted_queries = (
        frozen_step_queries.astype(jnp.float32)
        + ADAPTER_SCALE
        * jnp.dot(down_projection, adapter_up_map, preferred_element_type=jnp.float32)
    ).astype(jnp.bfloat16)
    q_pol = adapted_queries.reshape(rows_all, KVH, groups, HD)
    q_ref = frozen_step_queries.reshape(rows_all, KVH, groups, HD)
    rows = jnp.arange(rows_all, dtype=jnp.int32)
    seq = rows // half
    length_table = step_pair_lengths[0]
    prefix_length_value = prefix_length_table[0]
    mask_float = prefix_block_mask.astype(jnp.float32)
    nblocks = prefix_block_mask.shape[1]

    def prefix_visible(count):
        index = jnp.arange(count, dtype=jnp.int32)
        onehot = (
            jnp.arange(nblocks, dtype=jnp.int32)[:, None] == (index // BLOCK)[None, :]
        ).astype(jnp.float32)
        key_seen = (jnp.dot(mask_float, onehot) > 0.5) & (index < prefix_length_value)[None, :]
        return jnp.where((seq == 0)[:, None], key_seen[0][None, :], key_seen[1][None, :])

    step_seen = (seq[:, None] == seq[None, :]) & (rows[None, :] <= rows[:, None])

    def scores(query, keys):
        return (
            jnp.einsum(
                "tghd,kgd->tghk",
                query,
                keys.reshape(-1, KVH, HD),
                preferred_element_type=jnp.float32,
            )
            * factor
        )

    def update(state, query, keys, values, visible):
        peak_old, total_old, acc_old = state
        seen = visible[:, None, None, :]
        score = jnp.where(seen, scores(query, keys), NEG)
        peak_new = jnp.maximum(peak_old, jnp.max(score, axis=-1))
        rescale = jnp.exp(peak_old - peak_new)
        weights = jnp.where(seen, jnp.exp(score - peak_new[..., None]), 0.0)
        total_new = total_old * rescale + jnp.sum(weights, axis=-1)
        acc_new = acc_old * rescale[..., None] + jnp.einsum(
            "tghk,kgd->tghd",
            weights.astype(jnp.bfloat16),
            values.reshape(-1, KVH, HD),
            preferred_element_type=jnp.float32,
        )
        return (peak_new, total_new, acc_new)

    empty = (
        jnp.full((rows_all, KVH, groups), NEG, jnp.float32),
        jnp.zeros((rows_all, KVH, groups), jnp.float32),
        jnp.zeros((rows_all, KVH, groups, HD), jnp.float32),
    )
    state_pol = update(empty, q_pol, step_token_keys, step_token_values, step_seen)
    state_ref = update(empty, q_ref, step_token_keys, step_token_values, step_seen)
    whole_keys, whole_values = (
        lax.all_gather(prefix_key_table, "cont", axis=0, tiled=True),
        lax.all_gather(prefix_value_table, "cont", axis=0, tiled=True),
    )
    keys = whole_keys
    values = whole_values
    visible = prefix_visible(keys.shape[0])
    state_pol, state_ref = (
        update(state_pol, q_pol, keys, values, visible),
        update(state_ref, q_ref, keys, values, visible),
    )
    out_policy = state_pol[2] / state_pol[1][..., None]
    out_reference = state_ref[2] / state_ref[1][..., None]
    log_total = state_pol[0] + jnp.log(state_pol[1])
    read = readout.astype(jnp.float32)
    diff = (out_policy - out_reference).reshape(rows_all, QUERY_FEATURES)
    token_score = jnp.sum(diff * read[None, :], axis=1)
    seq_length = jnp.where(seq == 0, length_table[0], length_table[1])
    valid = rows - seq * half < seq_length
    margin = jnp.sum(jnp.where(valid, token_score, 0.0).reshape(2, half), axis=1)
    zvalue = BETA * (margin[0] - margin[1])
    loss = jax.nn.softplus(-zvalue)
    weight = BETA * jax.nn.sigmoid(-zvalue) * LOSS_SCALE
    d_margin = jnp.where(seq == 0, -weight, weight)
    d_out = (jnp.where(valid, d_margin, 0.0)[:, None] * read[None, :]).astype(jnp.bfloat16)
    d_heads = d_out.reshape(rows_all, KVH, groups, HD)
    row_dot = jnp.sum(d_heads.astype(jnp.float32) * out_policy, axis=-1)

    def grad_part(total, keys, values, visible):
        seen = visible[:, None, None, :]
        prob = jnp.where(seen, jnp.exp(scores(q_pol, keys) - log_total[..., None]), 0.0)
        d_weight = jnp.einsum(
            "tghd,kgd->tghk",
            d_heads,
            values.reshape(-1, KVH, HD),
            preferred_element_type=jnp.float32,
        )
        d_score = (prob * (d_weight - row_dot[..., None])).astype(jnp.bfloat16)
        return total + jnp.einsum(
            "tghk,kgd->tghd", d_score, keys.reshape(-1, KVH, HD), preferred_element_type=jnp.float32
        )

    d_acc = grad_part(
        jnp.zeros((rows_all, KVH, groups, HD), jnp.float32),
        step_token_keys,
        step_token_values,
        step_seen,
    )
    keys = whole_keys
    values = whole_values
    d_acc = grad_part(d_acc, keys, values, prefix_visible(keys.shape[0]))
    query_gradient = (d_acc * factor).astype(jnp.bfloat16).reshape(rows_all, QUERY_FEATURES)
    up_map_gradient = ADAPTER_SCALE * jnp.dot(
        down_projection.T, query_gradient, preferred_element_type=jnp.float32
    )
    down_gradient = (
        ADAPTER_SCALE
        * jnp.dot(query_gradient, adapter_up_map.T, preferred_element_type=jnp.float32)
    ).astype(jnp.bfloat16)
    grad_down = jnp.dot(down_gradient.T, tokens, preferred_element_type=jnp.float32)
    loss_total, grad_down, up_map_gradient = lax.psum(
        (loss, grad_down, up_map_gradient), ("dp", "cont")
    )
    return (loss_total, grad_down, up_map_gradient)


def solution(mesh):
    return jax.shard_map(
        local,
        mesh=mesh,
        in_specs=(
            P(("dp", "cont"), None),
            P(("dp", "cont"), None),
            P(("dp", "cont"), None),
            P(("dp", "cont"), None),
            P(("dp", "cont"), None),
            P(("dp", "cont"), None),
            P(),
            P(),
            P(),
            P(("dp", "cont"), None),
            P("dp"),
            P(("dp", "cont"), None),
        ),
        out_specs=(P(), P(), P()),
        check_vma=False,
    )
```

profile of v0, /device:TPU:1, one launch (start us, length us, event | category | flops | bytes accessed | tf_op | source)
XLA Modules:
  0.0 450.5 jit_solution(5731084654299776223)
XLA Ops:
  7.2 0.7 all-gather.3.cloned.1.call-update
  8.0 0.7 all-gather.5.cloned.1.call-update
  9.4 1.4 fusion.107
  10.8 0.8 fusion.74
  11.7 1.3 bitcast_convert_fusion
  13.1 1.0 copy.106
  14.1 0.2 copy.83
  14.3 1.9 copy.107
  16.2 1.6 convolution_convert_fusion
  17.8 0.7 fusion.70
  18.5 0.6 copy.105
  19.2 0.6 copy.108
  19.8 1.7 fusion.68
  21.5 0.1 broadcast_select_fusion
  21.6 1.9 copy-done.1
  23.5 4.6 %fusion.31 = (f32[128,8,8]{0,2,1:T(8,128)S(1)}, f32[128,8,8]{0,2,1:T(8,128)S(1)}, f32[8,128,128,8]{2,1,3,0:T(8,128)}) fusion(pred[128,128]{0,1:T(8,128)(4,1)S(1)} %fusion.79, f32[8,128,8,128]{1,3,2,0:T(8,128)S(1)} %fusion.68, bf16[128,8,128,1]{0,2,3,1:T(8,128)(2,1)S(1)} %copy.83, bf16[128,8,8,128]{3,2,1,0:T(8,128)(2,1)S(1)} %bitcast.175), kind=kOutput, calls=%fused_computation.50 | convolution fusion | flops 274710528 | bytes 10829824 | tf_op jit(solution)/shard_map/tghd,kgd->tghk/dot_general | solution.py:66
  28.1 36.8 %all-gather.3.cloned.1.call-done = bf16[512,1024]{1,0:T(8,128)(2,1)} async-done(((bf16[32,1024]{1,0:T(8,128)(2,1)}), bf16[512,1024]{1,0:T(8,128)(2,1)}) %all-gather.3.cloned.1.call-update) | async-done | bytes 1048592 | tf_op jit(solution)/shard_map/all_gather | solution.py:99
  65.0 1.5 copy.51
  66.5 9.9 %fusion.66 = f32[8,128,8,512]{3,1,2,0:T(8,128)} fusion(bf16[512,8,128,1]{0,2,3,1:T(8,128)(2,1)S(1)} %bitcast.177, bf16[128,8,8,128]{3,2,1,0:T(8,128)(2,1)} %bitcast.174), kind=kOutput, calls=%fused_computation.79 | convolution fusion | flops 1073741824 | bytes 19922944 | tf_op jit(solution)/shard_map/tghd,kgd->tghk/dot_general | solution.py:66
  76.4 13.2 %fusion.5 = (f32[128,8,8]{0,2,1:T(8,128)S(1)}, f32[128,8,8]{0,2,1:T(8,128)S(1)}, f32[8,512,128,8]{1,2,3,0:T(8,128)}) fusion(pred[128,512]{1,0:T(8,128)(4,1)S(1)} %broadcast_select_fusion, f32[8,128,8,512]{3,1,2,0:T(8,128)} %fusion.66, bf16[512,8,128,1]{0,2,3,1:T(8,128)(2,1)S(1)} %bitcast.178, bf16[128,8,8,128]{3,2,1,0:T(8,128)(2,1)S(1)} %bitcast.176), kind=kOutput, calls=%fused_computation.11 | convolution fusion | flops 1098891264 | bytes 36831232 | tf_op jit(solution)/shard_map/tghd,kgd->tghk/dot_general | solution.py:66
  89.6 0.7 exponential_multiply_fusion.1
  90.3 0.6 exponential_multiply_fusion
  90.9 0.6 copy-done.20
  91.6 15.4 %fusion.8 = (f32[128,8,8]{0,2,1:T(8,128)}, f32[128,8,8]{0,2,1:T(8,128)}) fusion(f32[8,512,128,8]{1,2,3,0:T(8,128)} %get-tuple-element.31, f32[128,8,8]{0,2,1:T(8,128)S(1)} %get-tuple-element.21, pred[128,512]{1,0:T(8,128)(4,1)S(1)} %broadcast_select_fusion, f32[128,8,8]{0,2,1:T(8,128)S(1)} %get-tuple-element.24, f32[8,128,8,512]{3,1,2,0:T(8,128)} %fusion.66), kind=kLoop, calls=%fused_computation.14 | loop fusion | flops 41926656 | bytes 33751040 | tf_op jit(solution)/shard_map/reduce_sum | solution.py:82
  107.0 9.4 %all-gather.5.cloned.1.call-done = bf16[512,1024]{1,0:T(8,128)(2,1)} async-done(((bf16[32,1024]{1,0:T(8,128)(2,1)}), bf16[512,1024]{1,0:T(8,128)(2,1)}) %all-gather.5.cloned.1.call-update) | async-done | bytes 1048592 | tf_op jit(solution)/shard_map/all_gather | solution.py:100
  116.4 2.3 copy.54
  118.7 9.8 %fusion.12 = f32[8,128,8,128]{1,3,2,0:T(8,128)} fusion(bf16[512,8,128,1]{0,2,3,1:T(8,128)(2,1)} %bitcast.183, f32[8,512,128,8]{1,2,3,0:T(8,128)} %get-tuple-element.31, f32[128,8,8]{0,2,1:T(8,128)} %copy-done.20, pred[128,512]{1,0:T(8,128)(4,1)S(1)} %broadcast_select_fusion), kind=kOutput, calls=%fused_computation.20 | convolution fusion | flops 1094713344 | bytes 22118400 | tf_op jit(solution)/shard_map/tghk,kgd->tghd/dot_general | solution.py:83
  128.6 9.6 %fusion.14 = f32[8,128,8,128]{1,3,2,0:T(8,128)S(1)} fusion(bf16[512,8,128,1]{0,2,3,1:T(8,128)(2,1)S(1)} %bitcast.185, f32[8,128,8,512]{3,1,2,0:T(8,128)} %fusion.66, f32[128,8,8]{0,2,1:T(8,128)S(1)} %copy-done.15, pred[128,512]{1,0:T(8,128)(4,1)S(1)} %broadcast_select_fusion), kind=kOutput, calls=%fused_computation.21 | convolution fusion | flops 1094713344 | bytes 22118400 | tf_op jit(solution)/shard_map/tghk,kgd->tghd/dot_general | solution.py:83
  138.2 2.3 fusion.34
  140.5 0.7 log_add_fusion
  141.2 1.7 fusion.24
  143.0 2.0 copy-done.8
  144.9 3.0 fusion.28
  148.0 0.7 reduce_sum.70
  148.7 1.4 fusion.86
  150.1 0.6 fusion.106
  152.0 1.3 compare_select_fusion
  153.3 0.5 copy-done.28
  153.8 2.9 multiply_reduce_fusion
  156.7 0.6 copy-done.25
  157.3 16.4 %fusion.36 = f32[8,128,8,128]{1,3,2,0:T(8,128)} fusion(bf16[512,8,128,1]{0,2,3,1:T(8,128)(2,1)S(1)} %bitcast.179, f32[8,128,8,512]{3,1,2,0:T(8,128)} %fusion.66, bf16[512,8,128,1]{0,2,3,1:T(8,128)(2,1)} %bitcast.184, f32[128,8,8]{0,2,1:T(8,128)S(1)} %multiply_reduce_fusion, f32[128,8,8]{0,2,1:T(8,128)} %get-tuple-element.15, ...), kind=kOutput, calls=%fused_computation.55 | convolution fusion | flops 2174746624 | bytes 23233024 | tf_op jit(solution)/shard_map/tghk,kgd->tghd/dot_general | solution.py:136
  173.7 6.5 %multiply_convert_fusion = bf16[8,128,8,128]{1,3,2,0:T(8,128)(2,1)} fusion(f32[8,128,8,128]{1,3,2,0:T(8,128)} %fusion.36, bf16[128,8,128,1]{0,2,3,1:T(8,128)(2,1)S(1)} %copy.83, f32[8,128,8,128]{1,3,2,0:T(8,128)} %copy-done.1, f32[128,8,8]{0,2,1:T(8,128)} %copy-done.25, f32[128]{0:T(128)} %copy-done.28, f32[128,8,8]{0,2,1:T(8,128)} %get-tuple-element.15, ...), kind=kOutput, calls=%fused_computation.42 | convolution fusion | flops 548405248 | bytes 11125248 | tf_op jit(solution)/shard_map/tghk,kgd->tghd/dot_general | solution.py:136
  180.2 3.0 convolution_multiply_fusion.1
  183.3 3.2 fusion.72
  186.5 76.1 %psum.21 = f32[]{:T(128)} all-reduce(f32[]{:T(128)S(6)} %select_n.140), channel_id=1, replica_groups=mesh['dp'=16,'cont'=16] {'dp','cont'}, use_global_device_ids=true, to_apply=%region_10.11 | all-reduce | flops 1 | bytes 8 | tf_op jit(solution)/shard_map/psum | solution.py:158
  262.7 177.5 %all-reduce.3.cloned.1.call-done = (f32[16,8192]{1,0:T(8,128)}, f32[16,8192]{1,0:T(8,128)}) async-done(((f32[16,8192]{1,0:T(8,128)}, f32[16,8192]{1,0:T(8,128)}), (f32[16,8192]{1,0:T(8,128)}, f32[16,8192]{1,0:T(8,128)})) %all-reduce.3.cloned.1.call-update) | async-done | bytes 1048592 | tf_op jit(solution)/shard_map/psum | solution.py:158
  440.2 1.9 copy.131
  442.1 1.9 copy.132
  (65 shorter events, 0.4 us)
Async XLA Ops:
  7.2 9.0 %copy-start = (bf16[128,8192]{1,0:T(8,128)(2,1)S(1)}, bf16[128,8192]{1,0:T(8,128)(2,1)}, u32[]{:S(2)}) copy-start(bf16[128,8192]{1,0:T(8,128)(2,1)} %param.12) | copy-start | bytes 6291460
  7.2 10.6 %copy-start.9 = (bf16[16,8192]{1,0:T(8,128)(2,1)S(1)}, bf16[16,8192]{1,0:T(8,128)(2,1)}, u32[]{:S(2)}) copy-start(bf16[16,8192]{1,0:T(8,128)(2,1)} %param.19) | copy-start | bytes 786436
  7.2 57.8 %all-gather.3.cloned.1.call-start = ((), (), s32[]{:S(2)}) async-start(), calls=%async_computation | async-start | bytes 1114112 | tf_op jit(solution)/shard_map/all_gather | solution.py:99
  7.9 108.5 %all-gather.5.cloned.1.call-start = ((), (), s32[]{:S(2)}) async-start(), calls=%async_computation.1 | async-start | bytes 1114112 | tf_op jit(solution)/shard_map/all_gather | solution.py:100
  8.7 431.5 %all-reduce.3.cloned.1.call-start = ((), (), s32[]{:S(2)}) async-start(), calls=%async_computation.2 | async-start | bytes 2097152 | tf_op jit(solution)/shard_map/psum | solution.py:158
  14.3 3.5 copy-start.7
  17.8 1.4 copy-start.23
  19.2 2.3 copy-start.3
  19.8 1.8 copy-start.4
  21.5 2.0 copy-start.1
  66.5 9.9 %copy-start.5 = (bf16[16,8,64,128]{3,2,1,0:T(8,128)(2,1)S(1)}, bf16[16,8,64,128]{3,2,1,0:T(8,128)(2,1)}, u32[]{:S(2)}) copy-start(bf16[16,8,64,128]{3,2,1,0:T(8,128)(2,1)} %copy-done.4) | copy-start | bytes 6291460
  89.6 0.7 copy-start.12
  90.3 0.7 copy-start.14
  90.9 0.6 copy-start.20
  118.7 9.8 %copy-start.11 = (bf16[512,1024]{0,1:T(8,128)(2,1)S(1)}, bf16[512,1024]{0,1:T(8,128)(2,1)}, u32[]{:S(2)}) copy-start(bf16[512,1024]{0,1:T(8,128)(2,1)} %copy.54) | copy-start | bytes 3145732
  118.7 9.8 %copy-start.15 = (f32[128,8,8]{0,2,1:T(8,128)S(1)}, f32[128,8,8]{0,2,1:T(8,128)}, u32[]{:S(2)}) copy-start(f32[128,8,8]{0,2,1:T(8,128)} %copy-done.14) | copy-start | bytes 98308
  128.5 9.6 %copy-start.2 = (f32[8,128,8,128]{1,3,2,0:T(8,128)S(1)}, f32[8,128,8,128]{1,3,2,0:T(8,128)}, u32[]{:S(2)}) copy-start(f32[8,128,8,128]{1,3,2,0:T(8,128)} %copy-done.1) | copy-start | bytes 12582916
  128.5 9.6 %copy-start.6 = (f32[8,128,128,8]{2,1,3,0:T(8,128)S(1)}, f32[8,128,128,8]{2,1,3,0:T(8,128)}, u32[]{:S(2)}) copy-start(f32[8,128,128,8]{2,1,3,0:T(8,128)} %get-tuple-element.30) | copy-start | bytes 12582916
  128.5 9.6 %copy-start.17 = (f32[128,8,8]{0,2,1:T(8,128)S(1)}, f32[128,8,8]{0,2,1:T(8,128)}, u32[]{:S(2)}) copy-start(f32[128,8,8]{0,2,1:T(8,128)} %get-tuple-element.22) | copy-start | bytes 98308
  128.5 9.6 %copy-start.18 = (f32[128,8,8]{0,2,1:T(8,128)S(1)}, f32[128,8,8]{0,2,1:T(8,128)}, u32[]{:S(2)}) copy-start(f32[128,8,8]{0,2,1:T(8,128)} %get-tuple-element.25) | copy-start | bytes 98308
  138.2 2.3 copy-start.13
  138.2 2.3 copy-start.21
  138.2 2.3 copy-start.22
  138.2 3.0 copy-start.16
  138.2 3.0 copy-start.27
  141.2 3.7 copy-start.19
  141.2 3.7 copy-start.26
  141.2 3.7 copy-start.29
  143.0 2.0 copy-start.8
  153.3 0.5 copy-start.28
  156.7 0.6 copy-start.25
  173.7 6.5 %copy-start.24 = (bf16[128,16]{0,1:T(8,128)(2,1)S(1)}, bf16[128,16]{0,1:T(8,128)(2,1)}, u32[]{:S(2)}) copy-start(bf16[128,16]{0,1:T(8,128)(2,1)} %copy-done.23) | copy-start | bytes 12292
  173.7 9.5 %copy-start.10 = (bf16[16,8192]{1,0:T(8,128)(2,1)S(1)}, bf16[16,8192]{1,0:T(8,128)(2,1)}, u32[]{:S(2)}) copy-start(bf16[16,8192]{1,0:T(8,128)(2,1)} %param.19) | copy-start | bytes 786436
Sparse Core Ops, SparseCore 0:
  10.8 54.1 all-gather.2
  67.7 48.6 all-gather.4
  186.6 253.5 all-reduce.2
where the time goes:
time: 452 us; the launch traced here: 450 us
  waiting for transfers between devices  225 us (50%)
  matrix products  85.7 us (19%)
  blocking collectives  76.1 us (17%)
  other arithmetic  26.7 us (6%)
  local copies, waits for them, and re-layouts  20.3 us (4%)
  between operations  16.3 us (4%)
    psum x1, waiting for transfers between devices, local(): lax.psum((loss, grad_down, up_map_gradient), ('dp', 'cont'))  178 us
    psum x1, blocking collectives, local(): lax.psum((loss, grad_down, up_map_gradient), ('dp', 'cont'))  76.1 us
    all_gather x1, waiting for transfers between devices, local(): lax.all_gather(prefix_key_table, 'cont', axis=0, tiled=True)  36.8 us
    dot_general x4, matrix products, scores(): jnp.einsum('tghd,kgd->tghk', query, keys.reshape(-1, KVH, HD), preferred_...  29.4 us
    dot_general x4, matrix products, update(): jnp.einsum('tghk,kgd->tghd', weights.astype(jnp.bfloat16), values.reshape...  24.1 us
    dot_general x2, matrix products, grad_part(): jnp.einsum('tghk,kgd->tghd', d_score, keys.reshape(-1, KVH, HD), preferre...  22.9 us
    reduce_sum x2, other arithmetic, update(): total_new = total_old * rescale + jnp.sum(weights, axis=-1)  17.7 us
    unnamed x66, local copies, waits for them, and re-layouts  13.5 us
  transfers between devices with their start and end apart: 3, of which 3 were waited for; matrix products, arithmetic and copies ran while one was open for 13% of the time, Pallas kernels for 0%

commit v1 on v0

v1 whole, which is shorter than its diff:
```python
import functools

import jax
import jax.numpy as jnp
from jax import lax
from jax.experimental import pallas as pl
from jax.experimental.pallas import tpu as pltpu
from jax.sharding import PartitionSpec as P

HQ = 64
KVH = 8
HD = 128
HPG = HQ // KVH
BLOCK = 32
STEP = 64
RANK = 16
FEATURES = 8192
GCOL = HPG * HD
LANES = HPG * STEP

NEG = -1e30
BETA = 0.1
ADAPTER_SCALE = 2.0
LOSS_SCALE = 1024.0
FACTOR = HD**-0.5
LOG2E = 1.4426950408889634

MESH = pl.DeviceIdType.MESH
f32 = jnp.float32
bf16 = jnp.bfloat16


def nn(a, b):
    return lax.dot_general(a, b, (((1,), (0,)), ((), ())), preferred_element_type=f32)


def nt(a, b):
    return lax.dot_general(a, b, (((1,), (1,)), ((), ())), preferred_element_type=f32)


def iota(shape, dim):
    return lax.broadcasted_iota(jnp.int32, shape, dim)


def kernel(
    dims,
    tokens_hbm, fq_hbm, sk_hbm, sv_hbm, kshard, vshard, dmap_hbm, up_hbm, rd, lens, plen, mask,
    grads, loss_out,
    tokens, fq, sk, sv, dmap, up, kv, shard, ubuf, zbuf, rs, zs, bias, dblk, lossbuf,
    local_sem, gsend, grecv, fsend, frecv, psend, precv, zsend, zrecv, asend, arecv,
    lsend, lrecv,
):
    n_cont, n_z, nch = dims
    n_plane = 2 * n_cont
    n_chip = n_cont // 2
    prefix = BLOCK * n_cont
    width = FEATURES // n_plane
    per = KVH // nch
    dp = lax.axis_index("dp")
    cont = lax.axis_index("cont")
    core = lax.rem(cont, 2)
    chip = cont // 2
    zi = dp // 2
    xlo = lax.rem(dp, 2)
    me = xlo * n_cont + cont

    def plane_dev(p):
        return {"dp": zi * 2 + p // n_cont, "cont": lax.rem(p, n_cont)}

    def z_dev(z):
        return {"dp": z * 2 + xlo, "cont": cont}

    loads = []
    for i, (src, dst) in enumerate(
        ((dmap_hbm, dmap), (tokens_hbm, tokens), (sk_hbm, sk), (sv_hbm, sv), (fq_hbm, fq), (up_hbm, up))
    ):
        cp = pltpu.make_async_copy(src, dst, local_sem.at[i])
        cp.start()
        loads.append(cp)
    ld_dmap, ld_tokens, ld_sk, ld_sv, ld_fq, ld_up = loads

    barrier = pltpu.get_barrier_semaphore()

    def greet_plane(k, carry):
        pl.semaphore_signal(
            barrier, inc=1, device_id=plane_dev(lax.rem(me + k, n_plane)), device_id_type=MESH
        )
        return carry

    def greet_z(k, carry):
        pl.semaphore_signal(barrier, inc=1, device_id=z_dev(lax.rem(zi + k, n_z)), device_id_type=MESH)
        return carry

    lax.fori_loop(1, n_plane, greet_plane, 0)
    lax.fori_loop(1, n_z, greet_z, 0)

    rdf = rd[...].astype(f32)
    r2 = jnp.concatenate(
        [rdf[(i // 2) * HPG : (i // 2 + 1) * HPG] for i in range(2 * KVH)], axis=0
    )
    r2 = r2.astype(bf16)
    row_g = iota((HD, HD), 0) // 16

    def rv_of(values):
        total = None
        for g in range(KVH):
            w = jnp.where(row_g == g, r2, jnp.zeros_like(r2))
            part = nt(values[:, g * HD : (g + 1) * HD], w)
            total = part if total is None else total + part
        high = total.astype(bf16).astype(f32)
        low = total - high
        part_of = lax.rem(iota(total.shape, 1) // HPG, 2)
        return jnp.where(part_of == 0, high, low).astype(bf16)

    shard[:, 0:HD] = rv_of(vshard[...])
    shard[:, HD:] = kshard[...]
    kv[core, chip] = shard[...]

    pl.semaphore_wait(barrier, n_plane - 1 + n_z - 1)

    bounds = [0] + [HD * (1 + per * (n + 1)) for n in range(nch)]

    def gather_copy(n, k, slot):
        cols = pl.ds(bounds[n], bounds[n + 1] - bounds[n])
        other = lax.rem(chip + k, n_chip)
        return pltpu.make_async_remote_copy(
            src_ref=shard.at[:, cols],
            dst_ref=kv.at[core, slot, :, cols],
            send_sem=gsend.at[n, k],
            recv_sem=grecv.at[n, slot],
            device_id={"cont": other * 2 + core},
            device_id_type=MESH,
        )

    for n in range(nch):

        def start_gather(k, carry, n=n):
            gather_copy(n, k, chip).start()
            return carry

        lax.fori_loop(1, n_chip, start_gather, 0)

    def forward_copy(n):
        cols = pl.ds(bounds[n], bounds[n + 1] - bounds[n])
        return pltpu.make_async_remote_copy(
            src_ref=kv.at[core, :, :, cols],
            dst_ref=kv.at[core, :, :, cols],
            send_sem=fsend.at[n],
            recv_sem=frecv.at[n],
            device_id={"cont": chip * 2 + (1 - core)},
            device_id_type=MESH,
        )

    def forward_wait(n):
        cols = pl.ds(bounds[n], bounds[n + 1] - bounds[n])
        return pltpu.make_async_remote_copy(
            src_ref=kv.at[core, :, :, cols],
            dst_ref=kv.at[1 - core, :, :, cols],
            send_sem=fsend.at[n],
            recv_sem=frecv.at[n],
            device_id={"cont": chip * 2 + (1 - core)},
            device_id_type=MESH,
        )

    def arrive(n):
        def one(k, carry):
            gather_copy(n, k, lax.rem(chip + n_chip - k, n_chip)).wait_recv()
            return carry

        lax.fori_loop(1, n_chip, one, 0)
        forward_copy(n).start()

    ld_dmap.wait()
    ld_tokens.wait()
    down_f = nt(tokens[...], dmap[...])
    down = down_f.astype(bf16)
    len0 = lens[0, 0]
    len1 = lens[0, 1]
    lane128 = iota((RANK, HD), 1)
    t128 = lax.rem(lane128, STEP)
    down_t = nt(dmap[...], tokens[...]).astype(bf16).astype(f32)
    swapped = pltpu.roll(down_t, STEP, 1)
    first_half = lane128 < STEP
    blk_mask = (iota((HD, LANES), 0) // RANK) == (iota((HD, LANES), 1) // STEP)
    for c in range(2):
        both = jnp.where(first_half, down_t, swapped) if c == 0 else jnp.where(first_half, swapped, down_t)
        signed = jnp.where(t128 < (len0 if c == 0 else len1), -both if c == 0 else both, 0.0)
        tiled = jnp.concatenate([jnp.concatenate([signed] * 4, axis=1)] * KVH, axis=0)
        dblk[c] = jnp.where(blk_mask, tiled, 0.0).astype(bf16)

    limit = plen[0]
    for c in range(2):
        for b in range(n_cont):
            block = 2 * (b % n_chip) + b // n_chip
            ok = (mask[c, block] > 0) & (block * BLOCK < limit)
            bias[c, pl.ds(b * BLOCK, BLOCK), :] = jnp.full((BLOCK, HD), jnp.where(ok, 0.0, NEG), f32)
    causal = jnp.where(
        iota((STEP, LANES), 0) > lax.rem(iota((STEP, LANES), 1), STEP), NEG, 0.0
    ).astype(f32)

    ld_sk.wait()
    ld_sv.wait()
    rvs = rv_of(sv[...])
    rvs_t = [rvs[c * STEP : (c + 1) * STEP].astype(f32).T.astype(bf16) for c in range(2)]

    ld_fq.wait()
    ld_up.wait()

    ones_p = jnp.ones((RANK, prefix), bf16)
    ones_s = jnp.ones((RANK, STEP), bf16)
    pick = lax.rem(iota((RANK, LANES), 0), HPG) == (iota((RANK, LANES), 1) // STEP)

    def group_step(g, carry):
        acc0, acc1, dd0, dd1 = carry
        col = pl.multiple_of(g * GCOL, GCOL)
        kcol = pl.multiple_of(g * HD, HD)
        fq_g = fq[:, pl.ds(col, GCOL)]
        up_g = up[:, pl.ds(col, GCOL)]
        qp_g = (fq_g.astype(f32) + ADAPTER_SCALE * nn(down, up_g)).astype(bf16)
        up_blk = jnp.concatenate([up_g[:, h * HD : (h + 1) * HD] for h in range(HPG)], axis=0)
        kp_g = kv[:, :, :, pl.ds(kcol + HD, HD)]
        kp_g = kp_g.reshape(prefix, HD)
        kp_t = kp_g.T
        rvp = kv[:, :, :, 0:HD].reshape(prefix, HD)
        rowi = iota((HD, LANES), 0)
        expand = ((rowi // 16 == g) & (lax.rem(rowi, HPG) == iota((HD, LANES), 1) // STEP)).astype(
            f32
        ).astype(bf16)
        rvx_p = nn(rvp, expand)
        pick16 = (iota((16, HD), 0) + g * 16 == iota((16, HD), 1)).astype(f32).astype(bf16)
        rvp_t = nt(pick16, rvp).astype(bf16)
        left_p = jnp.concatenate([rvp_t, ones_p], axis=0)
        accs = [acc0, acc1]
        dds = [dd0, dd1]
        u_total = None
        for c in range(2):
            rows = slice(c * STEP, (c + 1) * STEP)
            ks_c = sk[rows, pl.ds(kcol, HD)]
            left_s = jnp.concatenate([nt(pick16, rvs[rows]).astype(bf16), ones_s], axis=0)
            rvx_s = nn(rvs[rows], expand)
            bias_c = jnp.concatenate([bias[c]] * (LANES // HD), axis=1)
            outs = []
            for q_g in (qp_g, fq_g):
                q = jnp.concatenate([q_g[rows, h * HD : (h + 1) * HD] for h in range(HPG)], axis=0)
                s_p = nt(kp_g, q) + bias_c
                s_s = nt(ks_c, q) + causal
                peak = jnp.maximum(
                    jnp.max(s_p, axis=0, keepdims=True), jnp.max(s_s, axis=0, keepdims=True)
                )
                e_p = jnp.exp2((s_p - peak) * (FACTOR * LOG2E)).astype(bf16)
                e_s = jnp.exp2((s_s - peak) * (FACTOR * LOG2E)).astype(bf16)
                st = nn(left_p, e_p) + nn(left_s, e_s)
                total = st[16:17]
                o = jnp.sum(jnp.where(pick, st[0:16], 0.0), axis=0, keepdims=True) / total
                outs.append((e_p, e_s, total, o))
            (e_p, e_s, total, o), o_ref = outs[0], outs[1][3]
            accs[c] = accs[c] + (o - o_ref)
            ds_p = (e_p.astype(f32) * (rvx_p - o)).astype(bf16)
            ds_s = (e_s.astype(f32) * (rvx_s - o)).astype(bf16)
            dq = nn(kp_t, ds_p) + nn(ks_c.T, ds_s)
            dq = (dq * (FACTOR / total)).astype(bf16)
            u = nt(dblk[c], dq)
            u_total = u if u_total is None else u_total + u
            t = jnp.where(blk_mask, nn(up_blk, dq), 0.0)
            folded = t[0:RANK]
            for h in range(1, HPG):
                folded = folded + t[h * RANK : (h + 1) * RANK]
            dds[c] = dds[c] + folded
        for h in range(HPG):
            ubuf[:, pl.ds(col + h * HD, HD)] = u_total[h * RANK : (h + 1) * RANK]
        return accs[0], accs[1], dds[0], dds[1]

    zero_acc = jnp.zeros((1, LANES), f32)
    zero_dd = jnp.zeros((RANK, LANES), f32)
    carry = (zero_acc, zero_acc, zero_dd, zero_dd)
    arrive(0)
    for n in range(nch):
        if n + 1 < nch:
            arrive(n + 1)
        forward_wait(n).wait_recv()
        carry = lax.fori_loop(n * per, (n + 1) * per, group_step, carry)
    acc0, acc1, dd0, dd1 = carry

    tl = lax.rem(iota((1, LANES), 1), STEP)
    m0 = jnp.sum(jnp.where(tl < len0, acc0, 0.0), axis=1, keepdims=True)
    m1 = jnp.sum(jnp.where(tl < len1, acc1, 0.0), axis=1, keepdims=True)
    zv = BETA * (m0 - m1)
    small = jnp.exp(-jnp.abs(zv))
    loss = jnp.maximum(-zv, 0.0) + jnp.log1p(small)
    weight = (BETA * LOSS_SCALE) * jnp.where(zv >= 0.0, small, 1.0) / (1.0 + small)

    def fold(dd):
        x = dd[:, 0:HD]
        for i in range(1, LANES // HD):
            x = x + dd[:, i * HD : (i + 1) * HD]
        return x + pltpu.roll(x, STEP, 1)

    f0 = fold(dd0)
    f1 = fold(dd1)
    dd = jnp.where(
        first_half,
        jnp.where(t128 < len0, -f0, 0.0),
        jnp.where(t128 < len1, f1, 0.0),
    )
    dd = (ADAPTER_SCALE * dd).astype(bf16)

    def finish(i, carry):
        cols = pl.ds(pl.multiple_of(i * GCOL, GCOL), GCOL)
        zbuf[0:RANK, cols] = (nn(dd, tokens[:, cols]) * weight).astype(bf16)
        zbuf[RANK:, cols] = (ubuf[:, cols] * (ADAPTER_SCALE * weight)).astype(bf16)
        return carry

    lax.fori_loop(0, KVH, finish, 0)

    def plane_copy(k, slot):
        p = lax.rem(me + k, n_plane)
        return pltpu.make_async_remote_copy(
            src_ref=zbuf.at[:, pl.ds(pl.multiple_of(p * width, 128), width)],
            dst_ref=rs.at[slot],
            send_sem=psend.at[k],
            recv_sem=precv.at[slot],
            device_id=plane_dev(p),
            device_id_type=MESH,
        )

    def start_plane(k, carry):
        plane_copy(k, me).start()
        return carry

    lax.fori_loop(1, n_plane, start_plane, 0)

    n_sub = n_cont // 4
    n_rest = 2 * n_sub
    sub = lax.rem(cont, 4)
    rest = xlo * n_sub + cont // 4

    def loss_copy(stage, k, size):
        if stage == 0:
            mine = sub
            to = {"cont": (cont // 4) * 4 + lax.rem(sub + k, 4)}
        elif stage == 1:
            mine = zi
            to = z_dev(lax.rem(zi + k, n_z))
        else:
            mine = rest
            r = lax.rem(rest + k, n_rest)
            to = {"dp": zi * 2 + r // n_sub, "cont": lax.rem(r, n_sub) * 4 + sub}
        return mine, lambda slot: pltpu.make_async_remote_copy(
            src_ref=lossbuf.at[stage, mine],
            dst_ref=lossbuf.at[stage, slot],
            send_sem=lsend.at[stage, k],
            recv_sem=lrecv.at[stage, slot],
            device_id=to,
            device_id_type=MESH,
        )

    def loss_start(stage, size, value):
        mine = (sub, zi, rest)[stage]
        lossbuf[stage, mine] = value
        for k in range(1, size):
            loss_copy(stage, k, size)[1](mine).start()

    def loss_end(stage, size):
        for k in range(1, size):
            mine, make = loss_copy(stage, k, size)
            cp = make(lax.rem(mine + size - k, size))
            cp.wait_recv()
        out = lossbuf[stage, 0]
        for k in range(1, size):
            out = out + lossbuf[stage, k]
        return out

    loss_start(0, 4, jnp.broadcast_to(loss, (1, 128)))

    my_cols = pl.ds(pl.multiple_of(me * width, 128), width)
    rs[me] = zbuf[:, my_cols]

    def plane_sum(k, acc):
        slot = lax.rem(me + n_plane - k, n_plane)
        plane_copy(k, slot).wait_recv()
        return acc + rs[slot].astype(f32)

    acc = lax.fori_loop(1, n_plane, plane_sum, rs[me].astype(f32))

    zs[zi] = acc.astype(bf16)

    def z_copy(k, slot):
        return pltpu.make_async_remote_copy(
            src_ref=zs.at[zi],
            dst_ref=zs.at[slot],
            send_sem=zsend.at[k],
            recv_sem=zrecv.at[slot],
            device_id=z_dev(lax.rem(zi + k, n_z)),
            device_id_type=MESH,
        )

    for k in range(1, n_z):
        z_copy(k, zi).start()
    loss_start(1, n_z, loss_end(0, 4))
    for k in range(1, n_z):
        z_copy(k, lax.rem(zi + n_z - k, n_z)).wait_recv()
    acc = zs[0].astype(f32)
    for z in range(1, n_z):
        acc = acc + zs[z].astype(f32)
    grads[:, my_cols] = acc.astype(bf16)

    def all_copy(k, p):
        cols = pl.ds(pl.multiple_of(p * width, 128), width)
        return pltpu.make_async_remote_copy(
            src_ref=grads.at[:, cols],
            dst_ref=grads.at[:, cols],
            send_sem=asend.at[k],
            recv_sem=arecv.at[p],
            device_id=plane_dev(lax.rem(me + k, n_plane)),
            device_id_type=MESH,
        )

    def start_all(k, carry):
        all_copy(k, me).start()
        return carry

    lax.fori_loop(1, n_plane, start_all, 0)
    loss_start(2, n_rest, loss_end(1, n_z))

    def drain_gather(k, carry):
        for n in range(nch):
            gather_copy(n, k, chip).wait_send()
        return carry

    lax.fori_loop(1, n_chip, drain_gather, 0)
    for n in range(nch):
        forward_copy(n).wait_send()

    def drain_plane(k, carry):
        plane_copy(k, me).wait_send()
        return carry

    lax.fori_loop(1, n_plane, drain_plane, 0)
    for k in range(1, n_z):
        z_copy(k, zi).wait_send()

    loss_out[...] = loss_end(2, n_rest)

    def end_all(k, carry):
        all_copy(k, lax.rem(me + n_plane - k, n_plane)).wait_recv()
        return carry

    lax.fori_loop(1, n_plane, end_all, 0)

    def drain_all(k, carry):
        all_copy(k, me).wait_send()
        return carry

    lax.fori_loop(1, n_plane, drain_all, 0)
    for stage, size in ((0, 4), (1, n_z), (2, n_rest)):
        for k in range(1, size):
            mine, make = loss_copy(stage, k, size)
            make(mine).wait_send()


def local(n_cont, n_z, tokens, fq, sk, sv, kshard, vshard, dmap, up, readout, lens, plen, mask):
    nch = 4
    n_plane = 2 * n_cont
    n_chip = n_cont // 2
    width = FEATURES // n_plane
    rows = tokens.shape[0]
    prefix = BLOCK * n_cont
    n_rest = n_cont // 2
    cols = HD + KVH * HD
    anyspec = pl.BlockSpec(memory_space=pl.ANY)
    vspec = pl.BlockSpec(memory_space=pltpu.VMEM)
    sspec = pl.BlockSpec(memory_space=pltpu.SMEM)
    dma = pltpu.SemaphoreType.DMA
    grads, loss = pl.pallas_call(
        functools.partial(kernel, (n_cont, n_z, nch)),
        out_shape=(
            jax.ShapeDtypeStruct((2 * RANK, FEATURES), bf16),
            jax.ShapeDtypeStruct((1, 128), f32),
        ),
        in_specs=[anyspec] * 4 + [vspec] * 2 + [anyspec] * 2 + [vspec] + [sspec] * 3,
        out_specs=(vspec, vspec),
        scratch_shapes=[
            pltpu.VMEM((rows, FEATURES), bf16),
            pltpu.VMEM((rows, FEATURES), bf16),
            pltpu.VMEM((rows, KVH * HD), bf16),
            pltpu.VMEM((rows, KVH * HD), bf16),
            pltpu.VMEM((RANK, FEATURES), bf16),
            pltpu.VMEM((RANK, FEATURES), bf16),
            pltpu.VMEM((2, n_chip, BLOCK, cols), bf16),
            pltpu.VMEM((BLOCK, cols), bf16),
            pltpu.VMEM((RANK, FEATURES), f32),
            pltpu.VMEM((2 * RANK, FEATURES), bf16),
            pltpu.VMEM((n_plane, 2 * RANK, width), bf16),
            pltpu.VMEM((n_z, 2 * RANK, width), bf16),
            pltpu.VMEM((2, prefix, HD), f32),
            pltpu.VMEM((2, HD, LANES), bf16),
            pltpu.VMEM((3, max(4, n_z, n_rest), 1, 128), f32),
            dma((6,)),
            dma((nch, n_chip)),
            dma((nch, n_chip)),
            dma((nch,)),
            dma((nch,)),
            dma((n_plane,)),
            dma((n_plane,)),
            dma((n_z,)),
            dma((n_z,)),
            dma((n_plane,)),
            dma((n_plane,)),
            dma((3, max(4, n_z, n_rest))),
            dma((3, max(4, n_z, n_rest))),
        ],
        compiler_params=pltpu.CompilerParams(
            collective_id=0, has_side_effects=True, vmem_limit_bytes=60 * 1024 * 1024
        ),
    )(tokens, fq, sk, sv, kshard, vshard, dmap, up, readout.reshape(HQ, HD), lens, plen, mask)
    return loss[0, 0], grads[0:RANK].astype(f32), grads[RANK:].astype(f32)


def solution(mesh):
    return jax.shard_map(
        functools.partial(local, mesh.shape["cont"], mesh.shape["dp"] // 2),
        mesh=mesh,
        in_specs=(
            P(("dp", "cont"), None),
            P(("dp", "cont"), None),
            P(("dp", "cont"), None),
            P(("dp", "cont"), None),
            P(("dp", "cont"), None),
            P(("dp", "cont"), None),
            P(),
            P(),
            P(),
            P(("dp", "cont"), None),
            P("dp"),
            P(("dp", "cont"), None),
        ),
        out_specs=(P(), P(), P()),
        check_vma=False,
    )
```

time: 452 us -> 77.1 us (0.17)
  waiting for transfers between devices: 225 us -> 0 us
  matrix products: 85.7 us -> 0 us
  blocking collectives: 76.1 us -> 0 us
  Pallas kernels: 0 us -> 71.8 us
  other arithmetic: 26.7 us -> 2.07 us
  local copies, waits for them, and re-layouts: 20.3 us -> 0 us
  between operations: 16.3 us -> 3.05 us
    psum x1 -> x0, waiting for transfers between devices: 178 us -> none  [local(): lax.psum((loss, grad_down, up_map_gradient), ('dp', 'cont'))]
    dot_general x15 -> x0, matrix products: 85.7 us -> none  [the longest x4 29.4 us: scores(): jnp.einsum('tghd,kgd->tghk', query, keys.reshape(-1, KVH, HD), preferred_...]
    psum x1 -> x0, blocking collectives: 76.1 us -> none  [local(): lax.psum((loss, grad_down, up_map_gradient), ('dp', 'cont'))]
    pallas_call x0 -> x1, Pallas kernels: none -> 71.8 us  [local(): pl.pallas_call(functools.partial(kernel, (n_cont, n_z, nch)), out_shape=(...]
    all_gather x2 -> x0, waiting for transfers between devices: 46.3 us -> none  [the longest x1 36.8 us: local(): lax.all_gather(prefix_key_table, 'cont', axis=0, tiled=True)]
    reduce_sum x4 -> x0, other arithmetic: 22 us -> none  [the longest x2 17.7 us: update(): total_new = total_old * rescale + jnp.sum(weights, axis=-1)]
    unnamed x66 -> x0, local copies, waits for them, and re-layouts: 13.5 us -> none
  transfers between devices with their start and end apart: 3 -> 0, of which waited for: 3 -> 0; matrix products, arithmetic and copies ran while one was open for 13% -> 0% of each run, Pallas kernels for 0% -> 0%
where the time goes in v1:
time: 77.1 us; the launch traced here: 77 us
  Pallas kernels  71.8 us (93%)
  between operations  3.05 us (4%)
  other arithmetic  2.07 us (3%)
    pallas_call x1, Pallas kernels, local(): pl.pallas_call(functools.partial(kernel, (n_cont, n_z, nch)), out_shape=(...  71.8 us
    convert_element_type x1, other arithmetic, local(): return (loss[0, 0], grads[0:RANK].astype(f32), grads[RANK:].astype(f32))  2.07 us

profile of v1, /device:TPU:1, one launch (start us, length us, event | category | flops | bytes accessed | tf_op | source)
XLA Modules:
  0.0 77.0 jit_solution(1079671695677316207)
XLA Ops:
  1.3 71.8 %shard_map.139 = (bf16[32,8192]{1,0:T(8,128)(2,1)}, f32[1,128]{1,0:T(1,128)}) custom-call(bf16[128,8192]{1,0:T(8,128)(2,1)} %tokens_hbm.1, bf16[128,8192]{1,0:T(8,128)(2,1)} %fq_hbm.1, bf16[128,1024]{1,0:T(8,128)(2,1)} %sk_hbm.1, bf16[128,1024]{1,0:T(8,128)(2,1)} %sv_hbm.1, bf16[32,1024]{1,0:T(8,128)(2,1)} %kshard.1, bf16[32,1024]{1,0:T(8,128)(2,1)} %vshard.1, ...), custom_call_target="tpu_custom_call" | custom-call | tf_op jit(solution)/shard_map/pallas_call | solution.py:474
  73.1 2.1 %slice_convert_fusion = (f32[16,8192]{1,0:T(8,128)}, f32[16,8192]{1,0:T(8,128)}) fusion(bf16[32,8192]{1,0:T(8,128)(2,1)} %get-tuple-element.6), kind=kLoop, calls=%fused_computation | loop fusion | flops 262144 | bytes 1572864 | tf_op jit(solution)/shard_map/convert_element_type | solution.py:516

commit v2 on v0

v2 whole, which is shorter than its diff:
```python
import functools

import jax
import jax.numpy as jnp
from jax import lax
from jax.experimental import pallas as pl
from jax.experimental.pallas import tpu as pltpu
from jax.sharding import PartitionSpec as P

HQ = 64
KVH = 8
HD = 128
HPG = HQ // KVH
BLOCK = 32
STEP = 64
RANK = 16
FEATURES = 8192
GCOL = HPG * HD
LANES = HPG * STEP
HALF = LANES // 2

NEG = -1e30
BETA = 0.1
ADAPTER_SCALE = 2.0
LOSS_SCALE = 1024.0
FACTOR = HD**-0.5
LOG2E = 1.4426950408889634

MESH = pl.DeviceIdType.MESH
f32 = jnp.float32
bf16 = jnp.bfloat16


def nn(a, b):
    return lax.dot_general(a, b, (((1,), (0,)), ((), ())), preferred_element_type=f32)


def nt(a, b):
    return lax.dot_general(a, b, (((1,), (1,)), ((), ())), preferred_element_type=f32)


def iota(shape, dim):
    return lax.broadcasted_iota(jnp.int32, shape, dim)


def kernel(
    dims,
    tokens_hbm, fq_hbm, sk_hbm, sv_hbm, ks_hbm, vs_hbm, dmap_hbm, up_hbm, rd_hbm,
    lens_hbm, plen_hbm, mask_hbm,
    grads, loss_out,
    tokens, fq, sk, sv, dmap, up, vshard, rd, lens, plen, mask,
    kv, shard, ubuf, dbuf, ru, rdn, zu, zd, bias, rvf, rvs, gbuf, notes, znotes,
    local_sem, gsend, grecv, fsend, frecv, usend, urecv, dsend, drecv,
    zusend, zurecv, zdsend, zdrecv, ausend, aurecv, adsend, adrecv,
    nsend, nrecv, znsend, znrecv,
):
    n_cont, n_z = dims
    n_plane = 2 * n_cont
    n_chip = n_cont // 2
    prefix = BLOCK * n_cont
    width = FEATURES // n_plane
    dests = n_plane // KVH
    dp = lax.axis_index("dp")
    cont = lax.axis_index("cont")
    core = lax.rem(cont, 2)
    chip = cont // 2
    zi = dp // 2
    xlo = lax.rem(dp, 2)
    me = xlo * n_cont + cont

    def plane_dev(p):
        return {"dp": zi * 2 + p // n_cont, "cont": lax.rem(p, n_cont)}

    def z_dev(z):
        return {"dp": z * 2 + xlo, "cont": cont}

    barrier = pltpu.get_barrier_semaphore()

    def greet_plane(k, carry):
        pl.semaphore_signal(
            barrier, inc=1, device_id=plane_dev(lax.rem(me + k, n_plane)), device_id_type=MESH
        )
        return carry

    def greet_z(k, carry):
        pl.semaphore_signal(barrier, inc=1, device_id=z_dev(lax.rem(zi + k, n_z)), device_id_type=MESH)
        return carry

    lax.fori_loop(1, n_plane, greet_plane, 0)
    lax.fori_loop(1, n_z, greet_z, 0)

    loads = []
    for i, (src, dst) in enumerate(
        (
            (vs_hbm, vshard),
            (rd_hbm, rd),
            (ks_hbm, shard.at[:, HD:]),
            (dmap_hbm, dmap),
            (tokens_hbm, tokens),
            (sv_hbm, sv),
            (lens_hbm, lens),
            (plen_hbm, plen),
            (mask_hbm, mask),
            (fq_hbm, fq),
            (up_hbm, up),
            (sk_hbm, sk),
        )
    ):
        cp = pltpu.make_async_copy(src, dst, local_sem.at[i])
        cp.start()
        loads.append(cp)
    ld_vs, ld_rd, ld_ks, ld_dmap, ld_tokens, ld_sv, ld_lens, ld_plen, ld_mask, ld_fq, ld_up, ld_sk = loads

    ld_vs.wait()
    ld_rd.wait()
    rd2 = jnp.concatenate([rd[...], rd[...]], axis=0)
    row_g = lax.rem(iota((HD, HD), 0), HQ) // HPG

    def rv_of(values):
        total = None
        for g in range(KVH):
            w = jnp.where(row_g == g, rd2, jnp.zeros_like(rd2))
            part = nt(values[:, g * HD : (g + 1) * HD], w)
            total = part if total is None else total + part
        return total

    rv = rv_of(vshard[...])
    high = rv.astype(bf16).astype(f32)
    shard[:, 0:HD] = jnp.where(iota(rv.shape, 1) < HQ, high, rv - high).astype(bf16)
    ld_ks.wait()
    kv[core, chip] = shard[...]

    pl.semaphore_wait(barrier, n_plane - 1 + n_z - 1)

    def block_cols(n):
        return pl.ds(pl.multiple_of(n * HD, HD), HD)

    def gather_copy(n, k, slot):
        return pltpu.make_async_remote_copy(
            src_ref=shard.at[:, block_cols(n)],
            dst_ref=kv.at[core, slot, :, block_cols(n)],
            send_sem=gsend.at[n, k],
            recv_sem=grecv.at[n, slot],
            device_id={"cont": lax.rem(chip + k, n_chip) * 2 + core},
            device_id_type=MESH,
        )

    def issue(n):
        def one(k, carry):
            gather_copy(n, k, chip).start()
            return carry

        lax.fori_loop(1, n_chip, one, 0)

    def forward_copy(n, which):
        return pltpu.make_async_remote_copy(
            src_ref=kv.at[core, :, :, block_cols(n)],
            dst_ref=kv.at[which, :, :, block_cols(n)],
            send_sem=fsend.at[n],
            recv_sem=frecv.at[n],
            device_id={"cont": chip * 2 + (1 - core)},
            device_id_type=MESH,
        )

    def arrive(n):
        def one(k, carry):
            gather_copy(n, k, lax.rem(chip + n_chip - k, n_chip)).wait_recv()
            return carry

        lax.fori_loop(1, n_chip, one, 0)
        forward_copy(n, core).start()

    issue(0)
    issue(1)
    issue(2)

    ld_dmap.wait()
    ld_tokens.wait()
    down_t = nt(dmap[...], tokens[...]).astype(bf16)
    down = down_t.astype(f32).T.astype(bf16)
    ld_lens.wait()
    len0 = lens[0, 0]
    len1 = lens[0, 1]
    lane = iota((RANK, HD), 1)
    t_of = lax.rem(lane, STEP)
    sign = jnp.where(
        lane < STEP,
        jnp.where(t_of < len0, -1.0, 0.0),
        jnp.where(t_of < len1, 1.0, 0.0),
    ).astype(f32)
    down_signed = (down_t.astype(f32) * sign).astype(bf16)

    ld_plen.wait()
    ld_mask.wait()
    limit = plen[0]
    for c in range(2):
        for b in range(n_cont):
            block = 2 * (b % n_chip) + b // n_chip
            ok = (mask[c, block] > 0) & (block * BLOCK < limit)
            bias[c, pl.ds(b * BLOCK, BLOCK), :] = jnp.full((BLOCK, HD), jnp.where(ok, 0.0, NEG), f32)
    causal = jnp.where(iota((STEP, HD), 0) > lax.rem(iota((STEP, HD), 1), STEP), NEG, 0.0).astype(f32)
    causal = jnp.concatenate([causal] * (HALF // HD), axis=1)

    ld_sv.wait()
    rvs[...] = rv_of(sv[...])
    ld_fq.wait()
    ld_up.wait()
    ld_sk.wait()

    def up_copy(p, slot):
        return pltpu.make_async_remote_copy(
            src_ref=ubuf.at[:, pl.ds(pl.multiple_of(p * width, 128), width)],
            dst_ref=ru.at[slot],
            send_sem=usend.at[p],
            recv_sem=urecv.at[slot],
            device_id=plane_dev(p),
            device_id_type=MESH,
        )

    def group_step(g, carry):
        accs = list(carry[:4])
        dd = carry[4]

        @pl.when(g + 2 <= KVH)
        def _():
            arrive(g + 2)

        @pl.when(g + 3 <= KVH)
        def _():
            issue(g + 3)

        forward_copy(g + 1, 1 - core).wait_recv()

        col = pl.multiple_of(g * GCOL, GCOL)
        fq_g = fq[:, pl.ds(col, GCOL)]
        up_g = up[:, pl.ds(col, GCOL)]
        qp_g = (fq_g.astype(f32) + ADAPTER_SCALE * nn(down, up_g)).astype(bf16)
        kp = kv[:, :, :, block_cols(g + 1)].reshape(prefix, HD)
        kp_t = kp.T
        ks = sk[:, block_cols(g)]
        units = [(c, j) for c in range(2) for j in range(2)]

        def query_t(q_g, c, j):
            rows = slice(c * STEP, (c + 1) * STEP)
            parts = []
            for i in range(2):
                h = 4 * j + 2 * i
                parts.append(
                    jnp.concatenate(
                        [q_g[rows, h * HD : (h + 1) * HD], q_g[rows, (h + 1) * HD : (h + 2) * HD]], axis=0
                    ).T
                )
            return jnp.concatenate(parts, axis=1)

        def stage_a(c, j):
            ks_c = ks[c * STEP : (c + 1) * STEP]
            out = []
            for q_g in (qp_g, fq_g):
                q = query_t(q_g, c, j)
                out.append((nn(kp, q), nn(ks_c, q)))
            return out

        def expand(rows, j):
            parts = []
            for i in range(2):
                index = g * HPG + 4 * j + 2 * i + iota(rows.shape, 1) // STEP
                parts.append(jnp.take_along_axis(rows, index, axis=1))
            return jnp.concatenate(parts, axis=1)

        def softmax(s_p, s_s, bias_c, rv_p, rv_s):
            s_p = s_p + bias_c
            s_s = s_s + causal
            peak = jnp.maximum(jnp.max(s_p, axis=0, keepdims=True), jnp.max(s_s, axis=0, keepdims=True))
            e_p = jnp.exp2((s_p - peak) * (FACTOR * LOG2E))
            e_s = jnp.exp2((s_s - peak) * (FACTOR * LOG2E))
            total = jnp.sum(e_p, axis=0, keepdims=True) + jnp.sum(e_s, axis=0, keepdims=True)
            o = jnp.sum(e_p * rv_p, axis=0, keepdims=True) + jnp.sum(e_s * rv_s, axis=0, keepdims=True)
            inverse = 1.0 / total
            return e_p, e_s, inverse, o * inverse

        def stage_b(scores, c, j):
            bias_c = jnp.concatenate([bias[c]] * (HALF // HD), axis=1)
            rv_p = expand(rvf[...], j)
            rv_s = expand(rvs[c * STEP : (c + 1) * STEP], j)
            e_p, e_s, inverse, o = softmax(*scores[0], bias_c, rv_p, rv_s)
            o_ref = softmax(*scores[1], bias_c, rv_p, rv_s)[3]
            ds_p = (e_p * (rv_p - o)).astype(bf16)
            ds_s = (e_s * (rv_s - o)).astype(bf16)
            return ds_p, ds_s, inverse * FACTOR, o - o_ref

        def stage_c(ds_p, ds_s, scale, c, j):
            ks_t = ks[c * STEP : (c + 1) * STEP].T
            dq = ((nn(kp_t, ds_p) + nn(ks_t, ds_s)) * scale).astype(bf16)
            for i in range(2):
                h = 4 * j + 2 * i
                nat = dq[:, i * HD : (i + 1) * HD].T
                for k in range(2):
                    gbuf[pl.ds(c * STEP, STEP), (h + k) * HD : (h + k + 1) * HD] = nat[
                        k * STEP : (k + 1) * STEP
                    ]

        scores = {0: stage_a(*units[0])}
        for u in range(4):
            if u + 1 < 4:
                scores[u + 1] = stage_a(*units[u + 1])
            ds_p, ds_s, scale, diff = stage_b(scores.pop(u), *units[u])
            accs[u] = accs[u] + diff
            stage_c(ds_p, ds_s, scale, *units[u])

        gq = gbuf[...]
        ubuf[:, pl.ds(col, GCOL)] = nn(down_signed, gq).astype(bf16)
        dd = dd + nt(up_g, gq)
        for i in range(dests):
            p = g * dests + i

            @pl.when(p != me)
            def _(p=p):
                up_copy(p, me).start()

        return (*accs, dd)

    arrive(0)
    arrive(1)
    forward_copy(0, 1 - core).wait_recv()
    rvx = kv[:, :, :, 0:HD].reshape(prefix, HD).astype(f32)
    rvf[...] = rvx + pltpu.roll(rvx, HQ, 1)

    zero_acc = jnp.zeros((1, HALF), f32)
    carry = lax.fori_loop(0, KVH, group_step, (zero_acc,) * 4 + (jnp.zeros((RANK, HD), f32),))
    dd = carry[4]

    tl = lax.rem(iota((1, HALF), 1), STEP)
    m0 = jnp.sum(jnp.where(tl < len0, carry[0] + carry[1], 0.0), axis=1, keepdims=True)
    m1 = jnp.sum(jnp.where(tl < len1, carry[2] + carry[3], 0.0), axis=1, keepdims=True)
    zv = BETA * (m0 - m1)
    small = jnp.exp(-jnp.abs(zv))
    loss = jnp.maximum(-zv, 0.0) + jnp.log1p(small)
    weight = (BETA * LOSS_SCALE) * jnp.where(zv >= 0.0, small, 1.0) / (1.0 + small)

    def note_copy(k, slot):
        return pltpu.make_async_remote_copy(
            src_ref=notes.at[me],
            dst_ref=notes.at[slot],
            send_sem=nsend.at[k],
            recv_sem=nrecv.at[slot],
            device_id=plane_dev(lax.rem(me + k, n_plane)),
            device_id_type=MESH,
        )

    notes[me] = jnp.where(iota((1, HD), 1) < 64, loss, weight)

    def start_note(k, carry):
        note_copy(k, me).start()
        return carry

    lax.fori_loop(1, n_plane, start_note, 0)

    dd = (ADAPTER_SCALE * dd * sign).astype(bf16)

    def down_copy(p, slot):
        return pltpu.make_async_remote_copy(
            src_ref=dbuf.at[:, pl.ds(pl.multiple_of(p * width, 128), width)],
            dst_ref=rdn.at[slot],
            send_sem=dsend.at[p],
            recv_sem=drecv.at[slot],
            device_id=plane_dev(p),
            device_id_type=MESH,
        )

    def finish(i, carry):
        cols = pl.ds(pl.multiple_of(i * GCOL, GCOL), GCOL)
        dbuf[:, cols] = (nn(dd, tokens[:, cols]) * weight).astype(bf16)
        for k in range(dests):
            p = i * dests + k

            @pl.when(p != me)
            def _(p=p):
                down_copy(p, me).start()

        return carry

    lax.fori_loop(0, KVH, finish, 0)

    my_cols = pl.ds(pl.multiple_of(me * width, 128), width)

    def z_copies(buf, send, recv):
        def make(k, slot):
            return pltpu.make_async_remote_copy(
                src_ref=buf.at[zi],
                dst_ref=buf.at[slot],
                send_sem=send.at[k],
                recv_sem=recv.at[slot],
                device_id=z_dev(lax.rem(zi + k, n_z)),
                device_id_type=MESH,
            )

        def start():
            for k in range(1, n_z):
                make(k, zi).start()

        def end():
            for k in range(1, n_z):
                make(k, lax.rem(zi + n_z - k, n_z)).wait_recv()
            out = buf[0].astype(f32)
            for z in range(1, n_z):
                out = out + buf[z].astype(f32)
            return out

        def drain():
            for k in range(1, n_z):
                make(k, zi).wait_send()

        return start, end, drain

    def all_copies(row, send, recv):
        def make(k, p):
            part = grads.at[pl.ds(row, RANK), pl.ds(pl.multiple_of(p * width, 128), width)]
            return pltpu.make_async_remote_copy(
                src_ref=part,
                dst_ref=part,
                send_sem=send.at[k],
                recv_sem=recv.at[p],
                device_id=plane_dev(lax.rem(me + k, n_plane)),
                device_id_type=MESH,
            )

        def loop(step):
            def one(k, carry):
                step(k)
                return carry

            lax.fori_loop(1, n_plane, one, 0)

        def start():
            loop(lambda k: make(k, me).start())

        def end():
            loop(lambda k: make(k, lax.rem(me + n_plane - k, n_plane)).wait_recv())

        def drain():
            loop(lambda k: make(k, me).wait_send())

        return start, end, drain

    zu_start, zu_end, zu_drain = z_copies(zu, zusend, zurecv)
    zd_start, zd_end, zd_drain = z_copies(zd, zdsend, zdrecv)
    zn_start, zn_end, zn_drain = z_copies(znotes, znsend, znrecv)
    au_start, au_end, au_drain = all_copies(0, ausend, aurecv)
    ad_start, ad_end, ad_drain = all_copies(RANK, adsend, adrecv)

    def up_sum(k, acc):
        slot = lax.rem(me + n_plane - k, n_plane)
        note_copy(k, slot).wait_recv()
        up_copy(slot, slot).wait_recv()
        return acc + notes[slot][:, HD - 1 : HD] * ru[slot].astype(f32)

    acc = lax.fori_loop(1, n_plane, up_sum, weight * ubuf[:, my_cols].astype(f32))
    zu[zi] = (ADAPTER_SCALE * acc).astype(bf16)
    zu_start()

    def note_sum(p, acc):
        return acc + notes[p]

    znotes[zi] = lax.fori_loop(1, n_plane, note_sum, notes[0])
    zn_start()

    def down_sum(k, acc):
        slot = lax.rem(me + n_plane - k, n_plane)
        down_copy(slot, slot).wait_recv()
        return acc + rdn[slot].astype(f32)

    acc = lax.fori_loop(1, n_plane, down_sum, dbuf[:, my_cols].astype(f32))
    zd[zi] = acc.astype(bf16)
    zd_start()

    grads[pl.ds(0, RANK), my_cols] = zu_end().astype(bf16)
    au_start()
    loss_out[...] = zn_end()
    grads[pl.ds(RANK, RANK), my_cols] = zd_end().astype(bf16)
    ad_start()

    def drain_gather(k, carry):
        for n in range(KVH + 1):
            gather_copy(n, k, chip).wait_send()
        return carry

    lax.fori_loop(1, n_chip, drain_gather, 0)
    for n in range(KVH + 1):
        forward_copy(n, core).wait_send()

    def drain_plane(k, carry):
        p = lax.rem(me + k, n_plane)
        up_copy(p, me).wait_send()
        down_copy(p, me).wait_send()
        note_copy(k, me).wait_send()
        return carry

    lax.fori_loop(1, n_plane, drain_plane, 0)
    zu_drain()
    zd_drain()
    zn_drain()
    au_drain()
    au_end()
    ad_drain()
    ad_end()


def local(n_cont, n_z, tokens, fq, sk, sv, kshard, vshard, dmap, up, readout, lens, plen, mask):
    n_plane = 2 * n_cont
    n_chip = n_cont // 2
    width = FEATURES // n_plane
    rows = tokens.shape[0]
    prefix = BLOCK * n_cont
    cols = HD + KVH * HD
    anyspec = pl.BlockSpec(memory_space=pl.ANY)
    vspec = pl.BlockSpec(memory_space=pltpu.VMEM)
    dma = pltpu.SemaphoreType.DMA
    grads, loss = pl.pallas_call(
        functools.partial(kernel, (n_cont, n_z)),
        out_shape=(
            jax.ShapeDtypeStruct((2 * RANK, FEATURES), bf16),
            jax.ShapeDtypeStruct((1, 128), f32),
        ),
        in_specs=[anyspec] * 12,
        out_specs=(vspec, vspec),
        scratch_shapes=[
            pltpu.VMEM((rows, FEATURES), bf16),
            pltpu.VMEM((rows, FEATURES), bf16),
            pltpu.VMEM((rows, KVH * HD), bf16),
            pltpu.VMEM((rows, KVH * HD), bf16),
            pltpu.VMEM((RANK, FEATURES), bf16),
            pltpu.VMEM((RANK, FEATURES), bf16),
            pltpu.VMEM((BLOCK, KVH * HD), bf16),
            pltpu.VMEM((HQ, HD), bf16),
            pltpu.SMEM((1, 2), jnp.int32),
            pltpu.SMEM((1,), jnp.int32),
            pltpu.SMEM((2, n_cont), jnp.int32),
            pltpu.VMEM((2, n_chip, BLOCK, cols), bf16),
            pltpu.VMEM((BLOCK, cols), bf16),
            pltpu.VMEM((RANK, FEATURES), bf16),
            pltpu.VMEM((RANK, FEATURES), bf16),
            pltpu.VMEM((n_plane, RANK, width), bf16),
            pltpu.VMEM((n_plane, RANK, width), bf16),
            pltpu.VMEM((n_z, RANK, width), bf16),
            pltpu.VMEM((n_z, RANK, width), bf16),
            pltpu.VMEM((2, prefix, HD), f32),
            pltpu.VMEM((prefix, HD), f32),
            pltpu.VMEM((rows, HD), f32),
            pltpu.VMEM((rows, GCOL), bf16),
            pltpu.VMEM((n_plane, 1, 128), f32),
            pltpu.VMEM((n_z, 1, 128), f32),
            dma((12,)),
            dma((KVH + 1, n_chip)),
            dma((KVH + 1, n_chip)),
            dma((KVH + 1,)),
            dma((KVH + 1,)),
            *[dma((n_plane,))] * 4,
            *[dma((n_z,))] * 4,
            *[dma((n_plane,))] * 6,
            *[dma((n_z,))] * 2,
        ],
        compiler_params=pltpu.CompilerParams(
            collective_id=0, has_side_effects=True, vmem_limit_bytes=60 * 1024 * 1024
        ),
    )(tokens, fq, sk, sv, kshard, vshard, dmap, up, readout.reshape(HQ, HD), lens, plen, mask)
    return loss[0, 0], grads[RANK:].astype(f32), grads[0:RANK].astype(f32)


def solution(mesh):
    return jax.shard_map(
        functools.partial(local, mesh.shape["cont"], mesh.shape["dp"] // 2),
        mesh=mesh,
        in_specs=(
            P(("dp", "cont"), None),
            P(("dp", "cont"), None),
            P(("dp", "cont"), None),
            P(("dp", "cont"), None),
            P(("dp", "cont"), None),
            P(("dp", "cont"), None),
            P(),
            P(),
            P(),
            P(("dp", "cont"), None),
            P("dp"),
            P(("dp", "cont"), None),
        ),
        out_specs=(P(), P(), P()),
        check_vma=False,
    )
```

time: 452 us -> 82.4 us (0.18)
  waiting for transfers between devices: 225 us -> 0 us
  matrix products: 85.7 us -> 0 us
  Pallas kernels: 0 us -> 77.2 us
  blocking collectives: 76.1 us -> 0 us
  other arithmetic: 26.7 us -> 2.07 us
  local copies, waits for them, and re-layouts: 20.3 us -> 0 us
  between operations: 16.3 us -> 3.05 us
    psum x1 -> x0, waiting for transfers between devices: 178 us -> none  [local(): lax.psum((loss, grad_down, up_map_gradient), ('dp', 'cont'))]
    dot_general x15 -> x0, matrix products: 85.7 us -> none  [the longest x4 29.4 us: scores(): jnp.einsum('tghd,kgd->tghk', query, keys.reshape(-1, KVH, HD), preferred_...]
    pallas_call x0 -> x1, Pallas kernels: none -> 77.2 us  [local(): pl.pallas_call(functools.partial(kernel, (n_cont, n_z)), out_shape=(jax.S...]
    psum x1 -> x0, blocking collectives: 76.1 us -> none  [local(): lax.psum((loss, grad_down, up_map_gradient), ('dp', 'cont'))]
    all_gather x2 -> x0, waiting for transfers between devices: 46.3 us -> none  [the longest x1 36.8 us: local(): lax.all_gather(prefix_key_table, 'cont', axis=0, tiled=True)]
    reduce_sum x4 -> x0, other arithmetic: 22 us -> none  [the longest x2 17.7 us: update(): total_new = total_old * rescale + jnp.sum(weights, axis=-1)]
    unnamed x66 -> x0, local copies, waits for them, and re-layouts: 13.5 us -> none
  transfers between devices with their start and end apart: 3 -> 0, of which waited for: 3 -> 0; matrix products, arithmetic and copies ran while one was open for 13% -> 0% of each run, Pallas kernels for 0% -> 0%
where the time goes in v2:
time: 82.4 us; the launch traced here: 82.3 us
  Pallas kernels  77.2 us (94%)
  between operations  3.05 us (4%)
  other arithmetic  2.07 us (3%)
    pallas_call x1, Pallas kernels, local(): pl.pallas_call(functools.partial(kernel, (n_cont, n_z)), out_shape=(jax.S...  77.2 us
    convert_element_type x1, other arithmetic, local(): return (loss[0, 0], grads[RANK:].astype(f32), grads[0:RANK].astype(f32))  2.07 us

profile of v2, /device:TPU:1, one launch (start us, length us, event | category | flops | bytes accessed | tf_op | source)
XLA Modules:
  0.0 82.3 jit_solution(3585018688132836727)
XLA Ops:
  1.3 77.2 %shard_map.139 = (bf16[32,8192]{1,0:T(8,128)(2,1)}, f32[1,128]{1,0:T(1,128)}) custom-call(bf16[128,8192]{1,0:T(8,128)(2,1)} %tokens_hbm.1, bf16[128,8192]{1,0:T(8,128)(2,1)} %fq_hbm.1, bf16[128,1024]{1,0:T(8,128)(2,1)} %sk_hbm.1, bf16[128,1024]{1,0:T(8,128)(2,1)} %sv_hbm.1, bf16[32,1024]{1,0:T(8,128)(2,1)} %ks_hbm.1, bf16[32,1024]{1,0:T(8,128)(2,1)} %vs_hbm.1, ...), custom_call_target="tpu_custom_call" | custom-call | tf_op jit(solution)/shard_map/pallas_call | solution.py:518
  78.5 2.1 %slice_convert_fusion = (f32[16,8192]{1,0:T(8,128)}, f32[16,8192]{1,0:T(8,128)}) fusion(bf16[32,8192]{1,0:T(8,128)(2,1)} %get-tuple-element.6), kind=kLoop, calls=%fused_computation | loop fusion | flops 262144 | bytes 1572864 | tf_op jit(solution)/shard_map/convert_element_type | solution.py:566

commit v3 on v2

v3 whole, which is shorter than its diff:
```python
import functools

import jax
import jax.numpy as jnp
from jax import lax
from jax.experimental import pallas as pl
from jax.experimental.pallas import tpu as pltpu
from jax.sharding import PartitionSpec as P

HQ = 64
KVH = 8
HD = 128
HPG = HQ // KVH
BLOCK = 32
STEP = 64
RANK = 16
FEATURES = 8192
GCOL = HPG * HD
LANES = HPG * STEP
HALF = LANES // 2

NEG = -1e30
BETA = 0.1
ADAPTER_SCALE = 2.0
LOSS_SCALE = 1024.0
FACTOR = HD**-0.5
LOG2E = 1.4426950408889634

MESH = pl.DeviceIdType.MESH
f32 = jnp.float32
bf16 = jnp.bfloat16


def nn(a, b):
    return lax.dot_general(a, b, (((1,), (0,)), ((), ())), preferred_element_type=f32)


def nt(a, b):
    return lax.dot_general(a, b, (((1,), (1,)), ((), ())), preferred_element_type=f32)


def iota(shape, dim):
    return lax.broadcasted_iota(jnp.int32, shape, dim)


def kernel(
    dims,
    tokens_hbm, fq_hbm, sk_hbm, sv_hbm, ks_hbm, vs_hbm, dmap_hbm, up_hbm, rd_hbm,
    lens_hbm, plen_hbm, mask_hbm,
    grads, loss_out,
    tokens, fq, sk, sv, dmap, up, vshard, rd, lens, plen, mask,
    kv, shard, ubuf, dbuf, ru, rdn, zu, zd, qt, seen, rvf, rvs, gbuf, notes, znotes,
    local_sem, gsend, grecv, fsend, frecv, usend, urecv, dsend, drecv, nsend, nrecv,
    zusend, zurecv, zdsend, zdrecv, znsend, znrecv, ausend, aurecv, adsend, adrecv,
    susend, surecv, sdsend, sdrecv,
):
    n_cont, n_z = dims
    n_plane = 2 * n_cont
    n_chip = n_cont // 2
    prefix = BLOCK * n_cont
    width = FEATURES // n_plane
    dests = n_plane // KVH
    n_half = n_plane // 2
    dp = lax.axis_index("dp")
    cont = lax.axis_index("cont")
    core = lax.rem(cont, 2)
    chip = cont // 2
    zi = dp // 2
    xlo = lax.rem(dp, 2)
    place = xlo * n_chip + chip
    me = core * n_half + place

    def plane_dev(p):
        r = lax.rem(p, n_half)
        return {"dp": zi * 2 + r // n_chip, "cont": lax.rem(r, n_chip) * 2 + p // n_half}

    sibling = {"cont": chip * 2 + (1 - core)}

    def remote(src, dst, send, recv, to):
        return pltpu.make_async_remote_copy(
            src_ref=src, dst_ref=dst, send_sem=send, recv_sem=recv, device_id=to, device_id_type=MESH
        )

    def z_dev(z):
        return {"dp": z * 2 + xlo, "cont": cont}

    barrier = pltpu.get_barrier_semaphore()

    def greet_plane(k, carry):
        pl.semaphore_signal(
            barrier, inc=1, device_id=plane_dev(lax.rem(me + k, n_plane)), device_id_type=MESH
        )
        return carry

    def greet_z(k, carry):
        pl.semaphore_signal(barrier, inc=1, device_id=z_dev(lax.rem(zi + k, n_z)), device_id_type=MESH)
        return carry

    lax.fori_loop(1, n_plane, greet_plane, 0)
    lax.fori_loop(1, n_z, greet_z, 0)

    loads = []
    for i, (src, dst) in enumerate(
        (
            (vs_hbm, vshard),
            (rd_hbm, rd),
            (ks_hbm, shard.at[:, HD:]),
            (dmap_hbm, dmap),
            (tokens_hbm, tokens),
            (sv_hbm, sv),
            (lens_hbm, lens),
            (plen_hbm, plen),
            (mask_hbm, mask),
            (fq_hbm, fq),
            (up_hbm, up),
            (sk_hbm, sk),
        )
    ):
        cp = pltpu.make_async_copy(src, dst, local_sem.at[i])
        cp.start()
        loads.append(cp)
    ld_vs, ld_rd, ld_ks, ld_dmap, ld_tokens, ld_sv, ld_lens, ld_plen, ld_mask, ld_fq, ld_up, ld_sk = loads

    ld_vs.wait()
    ld_rd.wait()
    rd2 = jnp.concatenate([rd[...], rd[...]], axis=0)
    row_g = lax.rem(iota((HD, HD), 0), HQ) // HPG

    def rv_of(values):
        total = None
        for g in range(KVH):
            w = jnp.where(row_g == g, rd2, jnp.zeros_like(rd2))
            part = nt(values[:, g * HD : (g + 1) * HD], w)
            total = part if total is None else total + part
        return total

    rv = rv_of(vshard[...])
    high = rv.astype(bf16).astype(f32)
    shard[:, 0:HD] = jnp.where(iota(rv.shape, 1) < HQ, high, rv - high).astype(bf16)
    ld_ks.wait()
    kv[core, chip] = shard[...]

    pl.semaphore_wait(barrier, n_plane - 1 + n_z - 1)

    part_width = 3 * HD

    def part_cols(n):
        return pl.ds(pl.multiple_of(n * part_width, HD), part_width)

    def block_cols(n):
        return pl.ds(pl.multiple_of(n * HD, HD), HD)

    def issue(n):
        def one(k, carry):
            remote(
                shard.at[:, part_cols(n)],
                kv.at[core, chip, :, part_cols(n)],
                gsend.at[n],
                grecv.at[n],
                {"cont": lax.rem(chip + k, n_chip) * 2 + core},
            ).start()
            return carry

        lax.fori_loop(1, n_chip, one, 0)

    def forward_copy(n, which):
        part = kv.at[core, :, :, part_cols(n)]
        return remote(part, kv.at[which, :, :, part_cols(n)], fsend.at[n], frecv.at[n], sibling)

    def arrive(n):
        part = kv.at[core, pl.ds(0, n_chip - 1), :, part_cols(n)]
        remote(part, part, gsend.at[n], grecv.at[n], sibling).wait_recv()
        forward_copy(n, core).start()

    for n in range(3):
        issue(n)

    ld_dmap.wait()
    ld_tokens.wait()
    down_t = nt(dmap[...], tokens[...]).astype(bf16)
    down = down_t.astype(f32).T.astype(bf16)
    ld_lens.wait()
    len0 = lens[0, 0]
    len1 = lens[0, 1]
    lane = iota((RANK, HD), 1)
    t_of = lax.rem(lane, STEP)
    sign = jnp.where(
        lane < STEP,
        jnp.where(t_of < len0, -1.0, 0.0),
        jnp.where(t_of < len1, 1.0, 0.0),
    ).astype(f32)
    down_signed = (down_t.astype(f32) * sign).astype(bf16)

    ld_plen.wait()
    ld_mask.wait()
    limit = plen[0]
    for b in range(n_cont):
        block = 2 * (b % n_chip) + b // n_chip
        inside = block * BLOCK < limit
        fill = [jnp.where((mask[c, block] > 0) & inside, 0.0, NEG) for c in range(2)]
        col = iota((BLOCK, HD), 1)
        seen[pl.ds(b * BLOCK, BLOCK), :] = jnp.where(
            col == 0, fill[0], jnp.where(col == 1, fill[1], 0.0)
        ).astype(bf16)
    causal = jnp.where(iota((STEP, HD), 0) > lax.rem(iota((STEP, HD), 1), STEP), NEG, 0.0).astype(f32)
    causal = jnp.concatenate([causal] * (HALF // HD), axis=1)

    ld_sv.wait()
    rvs[...] = rv_of(sv[...])
    ld_fq.wait()
    ld_up.wait()
    ld_sk.wait()

    def prepare(g, carry):
        col = pl.multiple_of(g * GCOL, GCOL)
        frozen = fq[:, pl.ds(col, GCOL)].astype(f32) * (FACTOR * LOG2E)
        change = nn(down, up[:, pl.ds(col, GCOL)]) * (ADAPTER_SCALE * FACTOR * LOG2E)
        for s, q in enumerate(((frozen + change).astype(bf16), frozen.astype(bf16))):
            for c in range(2):
                rows = slice(c * STEP, (c + 1) * STEP)
                for h in range(0, HPG, 2):
                    pair = [q[rows, (h + i) * HD : (h + i + 1) * HD] for i in range(2)]
                    at = c * LANES + h * STEP
                    qt[s, g, :, at : at + HD] = jnp.concatenate(pair, axis=0).T
        return carry

    lax.fori_loop(0, KVH, prepare, 0)
    picks = [(iota((HD, HALF), 0) == c).astype(f32).astype(bf16) for c in range(2)]

    def up_copy(p):
        cols = pl.ds(pl.multiple_of(p * width, 128), width)
        return remote(ubuf.at[:, cols], ru.at[me], usend.at[0], urecv.at[0], plane_dev(p))

    def group_step(g, carry):
        accs = list(carry[:4])
        dd = carry[4]

        for n in (1, 2):

            @pl.when(g == 3 * n - 2)
            def _(n=n):
                arrive(n)

            @pl.when(g == 3 * n - 1)
            def _(n=n):
                forward_copy(n, 1 - core).wait_recv()

        col = pl.multiple_of(g * GCOL, GCOL)
        up_g = up[:, pl.ds(col, GCOL)]
        kp = kv[:, :, :, block_cols(g + 1)].reshape(prefix, HD)
        kp_seen = jnp.concatenate([kp, seen[...]], axis=1)
        kp_t = kp.T
        ks = sk[:, block_cols(g)]
        units = [(c, j) for c in range(2) for j in range(2)]

        def stage_a(c, j):
            ks_c = ks[c * STEP : (c + 1) * STEP]
            out = []
            for s in range(2):
                at = c * LANES + j * HALF
                q = qt[s, g, :, at : at + HALF]
                out.append((nn(kp_seen, jnp.concatenate([q, picks[c]], axis=0)), nn(ks_c, q)))
            return out

        def expand(rows, j):
            parts = []
            for i in range(2):
                index = g * HPG + 4 * j + 2 * i + iota(rows.shape, 1) // STEP
                parts.append(jnp.take_along_axis(rows, index, axis=1))
            return jnp.concatenate(parts, axis=1)

        def softmax(s_p, s_s, rv_p, rv_s):
            s_s = s_s + causal
            peak = jnp.maximum(jnp.max(s_p, axis=0, keepdims=True), jnp.max(s_s, axis=0, keepdims=True))
            e_p = jnp.exp2(s_p - peak)
            e_s = jnp.exp2(s_s - peak)
            total = jnp.sum(e_p, axis=0, keepdims=True) + jnp.sum(e_s, axis=0, keepdims=True)
            o = jnp.sum(e_p * rv_p, axis=0, keepdims=True) + jnp.sum(e_s * rv_s, axis=0, keepdims=True)
            inverse = 1.0 / total
            return e_p, e_s, inverse, o * inverse

        def stage_b(scores, c, j):
            rv_p = expand(rvf[...], j)
            rv_s = expand(rvs[c * STEP : (c + 1) * STEP], j)
            e_p, e_s, inverse, o = softmax(*scores[0], rv_p, rv_s)
            o_ref = softmax(*scores[1], rv_p, rv_s)[3]
            ds_p = (e_p * (rv_p - o)).astype(bf16)
            ds_s = (e_s * (rv_s - o)).astype(bf16)
            return ds_p, ds_s, inverse * FACTOR, o - o_ref

        def stage_c(ds_p, ds_s, scale, c, j):
            ks_t = ks[c * STEP : (c + 1) * STEP].T
            dq = ((nn(kp_t, ds_p) + nn(ks_t, ds_s)) * scale).astype(bf16)
            for i in range(2):
                h = 4 * j + 2 * i
                nat = dq[:, i * HD : (i + 1) * HD].T
                for k in range(2):
                    gbuf[pl.ds(c * STEP, STEP), (h + k) * HD : (h + k + 1) * HD] = nat[
                        k * STEP : (k + 1) * STEP
                    ]

        scores = {0: stage_a(*units[0])}
        for u in range(4):
            if u + 1 < 4:
                scores[u + 1] = stage_a(*units[u + 1])
            ds_p, ds_s, scale, diff = stage_b(scores.pop(u), *units[u])
            accs[u] = accs[u] + diff
            stage_c(ds_p, ds_s, scale, *units[u])

        gq = gbuf[...]
        ubuf[:, pl.ds(col, GCOL)] = nn(down_signed, gq).astype(bf16)
        dd = dd + nt(up_g, gq)
        for i in range(dests):
            p = g * dests + i

            @pl.when(p != me)
            def _(p=p):
                up_copy(p).start()

        return (*accs, dd)

    arrive(0)
    forward_copy(0, 1 - core).wait_recv()
    rvx = kv[:, :, :, 0:HD].reshape(prefix, HD).astype(f32)
    rvf[...] = rvx + pltpu.roll(rvx, HQ, 1)

    zero_acc = jnp.zeros((1, HALF), f32)
    carry = lax.fori_loop(0, KVH, group_step, (zero_acc,) * 4 + (jnp.zeros((RANK, HD), f32),))
    dd = carry[4]

    tl = lax.rem(iota((1, HALF), 1), STEP)
    m0 = jnp.sum(jnp.where(tl < len0, carry[0] + carry[1], 0.0), axis=1, keepdims=True)
    m1 = jnp.sum(jnp.where(tl < len1, carry[2] + carry[3], 0.0), axis=1, keepdims=True)
    zv = BETA * (m0 - m1)
    small = jnp.exp(-jnp.abs(zv))
    loss = jnp.maximum(-zv, 0.0) + jnp.log1p(small)
    weight = (BETA * LOSS_SCALE) * jnp.where(zv >= 0.0, small, 1.0) / (1.0 + small)

    notes[me] = jnp.where(iota((1, HD), 1) < 64, loss, weight)

    def start_note(k, carry):
        to = plane_dev(lax.rem(me + k, n_plane))
        remote(notes.at[me], notes.at[me], nsend.at[0], nrecv.at[0], to).start()
        return carry

    lax.fori_loop(1, n_plane, start_note, 0)

    dd = (ADAPTER_SCALE * dd * sign).astype(bf16)

    def down_copy(p):
        cols = pl.ds(pl.multiple_of(p * width, 128), width)
        return remote(dbuf.at[:, cols], rdn.at[me], dsend.at[0], drecv.at[0], plane_dev(p))

    def finish(i, carry):
        cols = pl.ds(pl.multiple_of(i * GCOL, GCOL), GCOL)
        dbuf[:, cols] = (nn(dd, tokens[:, cols]) * weight).astype(bf16)
        for k in range(dests):
            p = i * dests + k

            @pl.when(p != me)
            def _(p=p):
                down_copy(p).start()

        return carry

    lax.fori_loop(0, KVH, finish, 0)

    my_cols = pl.ds(pl.multiple_of(me * width, 128), width)

    def z_start(buf, send, recv):
        for k in range(1, n_z):
            remote(buf.at[zi], buf.at[zi], send, recv, z_dev(lax.rem(zi + k, n_z))).start()

    def z_end(buf, send, recv):
        others = buf.at[pl.ds(0, n_z - 1)]
        remote(others, others, send, recv, sibling).wait_recv()
        out = buf[0].astype(f32)
        for z in range(1, n_z):
            out = out + buf[z].astype(f32)
        return out

    def all_start(row, send, recv):
        part = grads.at[pl.ds(row, RANK), my_cols]

        def one(k, carry):
            to = plane_dev(core * n_half + lax.rem(place + k, n_half))
            remote(part, part, send, recv, to).start()
            return carry

        lax.fori_loop(1, n_half, one, 0)

    def half_of(row, which):
        return grads.at[
            pl.ds(row, RANK), pl.ds(pl.multiple_of(which * n_half * width, 128), n_half * width)
        ]

    def all_forward(row, recv, send, to_sibling):
        others = grads.at[pl.ds(row, RANK), pl.ds(0, (n_half - 1) * width)]
        remote(others, others, send, recv, sibling).wait_recv()
        remote(half_of(row, core), half_of(row, core), send, to_sibling, sibling).start()

    def all_end(row, send, to_sibling):
        remote(half_of(row, core), half_of(row, 1 - core), send, to_sibling, sibling).wait_recv()

    others = notes.at[pl.ds(0, n_plane - 1)]
    remote(others, others, nsend.at[0], nrecv.at[0], sibling).wait_recv()
    others = ru.at[pl.ds(0, n_plane - 1)]
    remote(others, others, usend.at[0], urecv.at[0], sibling).wait_recv()
    ru[me] = ubuf[:, my_cols]

    def up_sum(p, acc):
        return acc + notes[p][:, HD - 1 : HD] * ru[p].astype(f32)

    acc = lax.fori_loop(0, n_plane, up_sum, jnp.zeros((RANK, width), f32))
    zu[zi] = (ADAPTER_SCALE * acc).astype(bf16)
    z_start(zu, zusend.at[0], zurecv.at[0])

    def note_sum(p, acc):
        return acc + notes[p]

    znotes[zi] = lax.fori_loop(1, n_plane, note_sum, notes[0])
    z_start(znotes, znsend.at[0], znrecv.at[0])

    others = rdn.at[pl.ds(0, n_plane - 1)]
    remote(others, others, dsend.at[0], drecv.at[0], sibling).wait_recv()
    rdn[me] = dbuf[:, my_cols]

    def down_sum(p, acc):
        return acc + rdn[p].astype(f32)

    acc = lax.fori_loop(0, n_plane, down_sum, jnp.zeros((RANK, width), f32))
    zd[zi] = acc.astype(bf16)
    z_start(zd, zdsend.at[0], zdrecv.at[0])

    grads[pl.ds(0, RANK), my_cols] = z_end(zu, zusend.at[0], zurecv.at[0]).astype(bf16)
    all_start(0, ausend.at[0], aurecv.at[0])
    loss_out[...] = z_end(znotes, znsend.at[0], znrecv.at[0])
    grads[pl.ds(RANK, RANK), my_cols] = z_end(zd, zdsend.at[0], zdrecv.at[0]).astype(bf16)
    all_start(RANK, adsend.at[0], adrecv.at[0])

    all_forward(0, aurecv.at[0], susend.at[0], surecv.at[0])

    def sent(ref, sem):
        remote(ref, ref, sem, sem, sibling).wait_send()

    for n in range(3):
        sent(kv.at[core, pl.ds(0, n_chip - 1), :, part_cols(n)], gsend.at[n])
        sent(kv.at[core, :, :, part_cols(n)], fsend.at[n])
    sent(ru.at[pl.ds(0, n_plane - 1)], usend.at[0])
    sent(rdn.at[pl.ds(0, n_plane - 1)], dsend.at[0])
    sent(notes.at[pl.ds(0, n_plane - 1)], nsend.at[0])
    sent(zu.at[pl.ds(0, n_z - 1)], zusend.at[0])
    sent(zd.at[pl.ds(0, n_z - 1)], zdsend.at[0])
    sent(znotes.at[pl.ds(0, n_z - 1)], znsend.at[0])

    all_forward(RANK, adrecv.at[0], sdsend.at[0], sdrecv.at[0])
    for row, sem in ((0, ausend), (RANK, adsend)):
        sent(grads.at[pl.ds(row, RANK), pl.ds(0, (n_half - 1) * width)], sem.at[0])
    all_end(0, susend.at[0], surecv.at[0])
    all_end(RANK, sdsend.at[0], sdrecv.at[0])
    sent(half_of(0, core), susend.at[0])
    sent(half_of(RANK, core), sdsend.at[0])


def local(n_cont, n_z, tokens, fq, sk, sv, kshard, vshard, dmap, up, readout, lens, plen, mask):
    n_plane = 2 * n_cont
    n_chip = n_cont // 2
    width = FEATURES // n_plane
    rows = tokens.shape[0]
    prefix = BLOCK * n_cont
    cols = HD + KVH * HD
    anyspec = pl.BlockSpec(memory_space=pl.ANY)
    vspec = pl.BlockSpec(memory_space=pltpu.VMEM)
    dma = pltpu.SemaphoreType.DMA
    grads, loss = pl.pallas_call(
        functools.partial(kernel, (n_cont, n_z)),
        out_shape=(
            jax.ShapeDtypeStruct((2 * RANK, FEATURES), bf16),
            jax.ShapeDtypeStruct((1, 128), f32),
        ),
        in_specs=[anyspec] * 12,
        out_specs=(vspec, vspec),
        scratch_shapes=[
            pltpu.VMEM((rows, FEATURES), bf16),
            pltpu.VMEM((rows, FEATURES), bf16),
            pltpu.VMEM((rows, KVH * HD), bf16),
            pltpu.VMEM((rows, KVH * HD), bf16),
            pltpu.VMEM((RANK, FEATURES), bf16),
            pltpu.VMEM((RANK, FEATURES), bf16),
            pltpu.VMEM((BLOCK, KVH * HD), bf16),
            pltpu.VMEM((HQ, HD), bf16),
            pltpu.SMEM((1, 2), jnp.int32),
            pltpu.SMEM((1,), jnp.int32),
            pltpu.SMEM((2, n_cont), jnp.int32),
            pltpu.VMEM((2, n_chip, BLOCK, cols), bf16),
            pltpu.VMEM((BLOCK, cols), bf16),
            pltpu.VMEM((RANK, FEATURES), bf16),
            pltpu.VMEM((RANK, FEATURES), bf16),
            pltpu.VMEM((n_plane, RANK, width), bf16),
            pltpu.VMEM((n_plane, RANK, width), bf16),
            pltpu.VMEM((n_z, RANK, width), bf16),
            pltpu.VMEM((n_z, RANK, width), bf16),
            pltpu.VMEM((2, KVH, HD, 2 * LANES), bf16),
            pltpu.VMEM((prefix, HD), bf16),
            pltpu.VMEM((prefix, HD), f32),
            pltpu.VMEM((rows, HD), f32),
            pltpu.VMEM((rows, GCOL), bf16),
            pltpu.VMEM((n_plane, 1, 128), f32),
            pltpu.VMEM((n_z, 1, 128), f32),
            dma((12,)),
            *[dma((3,))] * 4,
            *[dma((1,))] * 20,
        ],
        compiler_params=pltpu.CompilerParams(
            collective_id=0, has_side_effects=True, vmem_limit_bytes=60 * 1024 * 1024
        ),
    )(tokens, fq, sk, sv, kshard, vshard, dmap, up, readout.reshape(HQ, HD), lens, plen, mask)
    return loss[0, 0], grads[RANK:].astype(f32), grads[0:RANK].astype(f32)


def solution(mesh):
    return jax.shard_map(
        functools.partial(local, mesh.shape["cont"], mesh.shape["dp"] // 2),
        mesh=mesh,
        in_specs=(
            P(("dp", "cont"), None),
            P(("dp", "cont"), None),
            P(("dp", "cont"), None),
            P(("dp", "cont"), None),
            P(("dp", "cont"), None),
            P(("dp", "cont"), None),
            P(),
            P(),
            P(),
            P(("dp", "cont"), None),
            P("dp"),
            P(("dp", "cont"), None),
        ),
        out_specs=(P(), P(), P()),
        check_vma=False,
    )
```

time: 82.4 us -> 66 us (0.80)
  Pallas kernels: 77.2 us -> 60.7 us
    pallas_call x1, Pallas kernels: 77.2 us -> 60.7 us  [local(): pl.pallas_call(functools.partial(kernel, (n_cont, n_z)), out_shape=(jax.S...]
where the time goes in v3:
time: 66 us; the launch traced here: 65.8 us
  Pallas kernels  60.7 us (92%)
  between operations  3.05 us (5%)
  other arithmetic  2.07 us (3%)
    pallas_call x1, Pallas kernels, local(): pl.pallas_call(functools.partial(kernel, (n_cont, n_z)), out_shape=(jax.S...  60.7 us
    convert_element_type x1, other arithmetic, local(): return (loss[0, 0], grads[RANK:].astype(f32), grads[0:RANK].astype(f32))  2.07 us

profile of v3, /device:TPU:1, one launch (start us, length us, event | category | flops | bytes accessed | tf_op | source)
XLA Modules:
  0.0 65.8 jit_solution(10380865129256937053)
XLA Ops:
  1.3 60.7 %shard_map.139 = (bf16[32,8192]{1,0:T(8,128)(2,1)}, f32[1,128]{1,0:T(1,128)}) custom-call(bf16[128,8192]{1,0:T(8,128)(2,1)} %tokens_hbm.1, bf16[128,8192]{1,0:T(8,128)(2,1)} %fq_hbm.1, bf16[128,1024]{1,0:T(8,128)(2,1)} %sk_hbm.1, bf16[128,1024]{1,0:T(8,128)(2,1)} %sv_hbm.1, bf16[32,1024]{1,0:T(8,128)(2,1)} %ks_hbm.1, bf16[32,1024]{1,0:T(8,128)(2,1)} %vs_hbm.1, ...), custom_call_target="tpu_custom_call" | custom-call | tf_op jit(solution)/shard_map/pallas_call | solution.py:475
  62.0 2.1 %slice_convert_fusion = (f32[16,8192]{1,0:T(8,128)}, f32[16,8192]{1,0:T(8,128)}) fusion(bf16[32,8192]{1,0:T(8,128)(2,1)} %get-tuple-element.6), kind=kLoop, calls=%fused_computation | loop fusion | flops 262144 | bytes 1572864 | tf_op jit(solution)/shard_map/convert_element_type | solution.py:518

commit v4 on v3

--- a/solution.py
+++ b/solution.py
@@ -49,7 +49,7 @@
     lens_hbm, plen_hbm, mask_hbm,
     grads, loss_out,
     tokens, fq, sk, sv, dmap, up, vshard, rd, lens, plen, mask,
-    kv, shard, ubuf, dbuf, ru, rdn, zu, zd, qt, seen, rvf, rvs, gbuf, notes, znotes,
+    kv, shard, ubuf, dbuf, ru, rdn, zu, zd, qt, seen, picks, rvf, rvs, sbuf, mbuf, gbuf, notes, znotes,
     local_sem, gsend, grecv, fsend, frecv, usend, urecv, dsend, drecv, nsend, nrecv,
     zusend, zurecv, zdsend, zdrecv, znsend, znrecv, ausend, aurecv, adsend, adrecv,
     susend, surecv, sdsend, sdrecv,
@@ -172,8 +172,7 @@
         remote(part, part, gsend.at[n], grecv.at[n], sibling).wait_recv()
         forward_copy(n, core).start()
 
-    for n in range(3):
-        issue(n)
+    issue(0)
 
     ld_dmap.wait()
     ld_tokens.wait()
@@ -207,6 +206,7 @@
 
     ld_sv.wait()
     rvs[...] = rv_of(sv[...])
+    issue(1)
     ld_fq.wait()
     ld_up.wait()
     ld_sk.wait()
@@ -225,91 +225,76 @@
         return carry
 
     lax.fori_loop(0, KVH, prepare, 0)
-    picks = [(iota((HD, HALF), 0) == c).astype(f32).astype(bf16) for c in range(2)]
+    issue(2)
+    for c in range(2):
+        picks[c] = (iota((HD, HALF), 0) == c).astype(f32).astype(bf16)
 
     def up_copy(p):
         cols = pl.ds(pl.multiple_of(p * width, 128), width)
         return remote(ubuf.at[:, cols], ru.at[me], usend.at[0], urecv.at[0], plane_dev(p))
 
-    def group_step(g, carry):
-        accs = list(carry[:4])
-        dd = carry[4]
-
-        for n in (1, 2):
-
-            @pl.when(g == 3 * n - 2)
-            def _(n=n):
-                arrive(n)
-
-            @pl.when(g == 3 * n - 1)
-            def _(n=n):
-                forward_copy(n, 1 - core).wait_recv()
-
+    units = [(c, j) for c in range(2) for j in range(2)]
+
+    def stage_a(g, u, slot):
+        c, j = units[u]
+        kp = kv[:, :, :, block_cols(g + 1)].reshape(prefix, HD)
+        ks = sk[pl.ds(c * STEP, STEP), block_cols(g)]
+        at = c * LANES + j * HALF
+        for s in range(2):
+            q = qt[s, g, :, at : at + HALF]
+            s_p = nn(jnp.concatenate([kp, seen[...]], axis=1), jnp.concatenate([q, picks[c]], axis=0))
+            s_s = nn(ks, q) + causal
+            sbuf[slot, s, pl.ds(0, prefix), :] = s_p
+            sbuf[slot, s, pl.ds(prefix, STEP), :] = s_s
+            mbuf[slot, s] = jnp.maximum(
+                jnp.max(s_p, axis=0, keepdims=True), jnp.max(s_s, axis=0, keepdims=True)
+            )
+
+    def expand(rows, g, j):
+        parts = []
+        for i in range(2):
+            index = g * HPG + 4 * j + 2 * i + iota(rows.shape, 1) // STEP
+            parts.append(jnp.take_along_axis(rows, index, axis=1))
+        return jnp.concatenate(parts, axis=1)
+
+    def softmax(slot, s, rv_p, rv_s):
+        peak = mbuf[slot, s]
+        e_p = jnp.exp2(sbuf[slot, s, pl.ds(0, prefix), :] - peak)
+        e_s = jnp.exp2(sbuf[slot, s, pl.ds(prefix, STEP), :] - peak)
+        total = jnp.sum(e_p, axis=0, keepdims=True) + jnp.sum(e_s, axis=0, keepdims=True)
+        o = jnp.sum(e_p * rv_p, axis=0, keepdims=True) + jnp.sum(e_s * rv_s, axis=0, keepdims=True)
+        inverse = 1.0 / total
+        return e_p, e_s, inverse, o * inverse
+
+    def stage_b(g, u, slot):
+        c, j = units[u]
+        rv_p = expand(rvf[...], g, j)
+        rv_s = expand(rvs[pl.ds(c * STEP, STEP), :], g, j)
+        e_p, e_s, inverse, o = softmax(slot, 0, rv_p, rv_s)
+        ds_p = (e_p * (rv_p - o)).astype(bf16)
+        ds_s = (e_s * (rv_s - o)).astype(bf16)
+        o_ref = softmax(slot, 1, rv_p, rv_s)[3]
+        return ds_p, ds_s, inverse * FACTOR, o - o_ref
+
+    def stage_c(g, u, kp_t, ds_p, ds_s, scale):
+        c, j = units[u]
+        ks_t = sk[pl.ds(c * STEP, STEP), block_cols(g)].T
+        dq = ((nn(kp_t, ds_p) + nn(ks_t, ds_s)) * scale).astype(bf16)
+        for i in range(2):
+            h = 4 * j + 2 * i
+            nat = dq[:, i * HD : (i + 1) * HD].T
+            for k in range(2):
+                gbuf[pl.ds(c * STEP, STEP), (h + k) * HD : (h + k + 1) * HD] = nat[
+                    k * STEP : (k + 1) * STEP
+                ]
+
+    def tail(g, dd):
         col = pl.multiple_of(g * GCOL, GCOL)
-        up_g = up[:, pl.ds(col, GCOL)]
-        kp = kv[:, :, :, block_cols(g + 1)].reshape(prefix, HD)
-        kp_seen = jnp.concatenate([kp, seen[...]], axis=1)
-        kp_t = kp.T
-        ks = sk[:, block_cols(g)]
-        units = [(c, j) for c in range(2) for j in range(2)]
-
-        def stage_a(c, j):
-            ks_c = ks[c * STEP : (c + 1) * STEP]
-            out = []
-            for s in range(2):
-                at = c * LANES + j * HALF
-                q = qt[s, g, :, at : at + HALF]
-                out.append((nn(kp_seen, jnp.concatenate([q, picks[c]], axis=0)), nn(ks_c, q)))
-            return out
-
-        def expand(rows, j):
-            parts = []
-            for i in range(2):
-                index = g * HPG + 4 * j + 2 * i + iota(rows.shape, 1) // STEP
-                parts.append(jnp.take_along_axis(rows, index, axis=1))
-            return jnp.concatenate(parts, axis=1)
-
-        def softmax(s_p, s_s, rv_p, rv_s):
-            s_s = s_s + causal
-            peak = jnp.maximum(jnp.max(s_p, axis=0, keepdims=True), jnp.max(s_s, axis=0, keepdims=True))
-            e_p = jnp.exp2(s_p - peak)
-            e_s = jnp.exp2(s_s - peak)
-            total = jnp.sum(e_p, axis=0, keepdims=True) + jnp.sum(e_s, axis=0, keepdims=True)
-            o = jnp.sum(e_p * rv_p, axis=0, keepdims=True) + jnp.sum(e_s * rv_s, axis=0, keepdims=True)
-            inverse = 1.0 / total
-            return e_p, e_s, inverse, o * inverse
-
-        def stage_b(scores, c, j):
-            rv_p = expand(rvf[...], j)
-            rv_s = expand(rvs[c * STEP : (c + 1) * STEP], j)
-            e_p, e_s, inverse, o = softmax(*scores[0], rv_p, rv_s)
-            o_ref = softmax(*scores[1], rv_p, rv_s)[3]
-            ds_p = (e_p * (rv_p - o)).astype(bf16)
-            ds_s = (e_s * (rv_s - o)).astype(bf16)
-            return ds_p, ds_s, inverse * FACTOR, o - o_ref
-
-        def stage_c(ds_p, ds_s, scale, c, j):
-            ks_t = ks[c * STEP : (c + 1) * STEP].T
-            dq = ((nn(kp_t, ds_p) + nn(ks_t, ds_s)) * scale).astype(bf16)
-            for i in range(2):
-                h = 4 * j + 2 * i
-                nat = dq[:, i * HD : (i + 1) * HD].T
-                for k in range(2):
-                    gbuf[pl.ds(c * STEP, STEP), (h + k) * HD : (h + k + 1) * HD] = nat[
-                        k * STEP : (k + 1) * STEP
-                    ]
-
-        scores = {0: stage_a(*units[0])}
-        for u in range(4):
-            if u + 1 < 4:
-                scores[u + 1] = stage_a(*units[u + 1])
-            ds_p, ds_s, scale, diff = stage_b(scores.pop(u), *units[u])
-            accs[u] = accs[u] + diff
-            stage_c(ds_p, ds_s, scale, *units[u])
-
         gq = gbuf[...]
         ubuf[:, pl.ds(col, GCOL)] = nn(down_signed, gq).astype(bf16)
-        dd = dd + nt(up_g, gq)
+        return dd + nt(up[:, pl.ds(col, GCOL)], gq)
+
+    def send_up(g):
         for i in range(dests):
             p = g * dests + i
 
@@ -317,6 +302,33 @@
             def _(p=p):
                 up_copy(p).start()
 
+    def group_step(g, carry):
+        accs = list(carry[:4])
+
+        for n in (1, 2):
+
+            @pl.when(g == 3 * n - 3)
+            def _(n=n):
+                arrive(n)
+
+            @pl.when(g == 3 * n - 2)
+            def _(n=n):
+                forward_copy(n, 1 - core).wait_recv()
+
+        @pl.when(g >= 2)
+        def _():
+            send_up(g - 2)
+
+        dd = tail(jnp.maximum(g - 1, 0), carry[4])
+        kp_t = kv[:, :, :, block_cols(g + 1)].reshape(prefix, HD).T
+        for u in range(4):
+            if u < 3:
+                stage_a(g, u + 1, (u + 1) % 2)
+            else:
+                stage_a(jnp.minimum(g + 1, KVH - 1), 0, 0)
+            ds_p, ds_s, scale, diff = stage_b(g, u, u % 2)
+            accs[u] = accs[u] + diff
+            stage_c(g, u, kp_t, ds_p, ds_s, scale)
         return (*accs, dd)
 
     arrive(0)
@@ -324,9 +336,13 @@
     rvx = kv[:, :, :, 0:HD].reshape(prefix, HD).astype(f32)
     rvf[...] = rvx + pltpu.roll(rvx, HQ, 1)
 
+    gbuf[...] = jnp.zeros_like(gbuf)
+    stage_a(0, 0, 0)
     zero_acc = jnp.zeros((1, HALF), f32)
     carry = lax.fori_loop(0, KVH, group_step, (zero_acc,) * 4 + (jnp.zeros((RANK, HD), f32),))
-    dd = carry[4]
+    send_up(KVH - 2)
+    dd = tail(KVH - 1, carry[4])
+    send_up(KVH - 1)
 
     tl = lax.rem(iota((1, HALF), 1), STEP)
     m0 = jnp.sum(jnp.where(tl < len0, carry[0] + carry[1], 0.0), axis=1, keepdims=True)
@@ -336,34 +352,27 @@
     loss = jnp.maximum(-zv, 0.0) + jnp.log1p(small)
     weight = (BETA * LOSS_SCALE) * jnp.where(zv >= 0.0, small, 1.0) / (1.0 + small)
 
-    notes[me] = jnp.where(iota((1, HD), 1) < 64, loss, weight)
+    notes[me] = jnp.where(iota((2, HD), 0) == 0, loss, weight)
 
     def start_note(k, carry):
         to = plane_dev(lax.rem(me + k, n_plane))
         remote(notes.at[me], notes.at[me], nsend.at[0], nrecv.at[0], to).start()
         return carry
 
+    dd = (ADAPTER_SCALE * dd * sign).astype(bf16)
+    for i in range(KVH):
+        cols = pl.ds(i * GCOL, GCOL)
+        dbuf[:, cols] = nn(dd, tokens[:, cols]).astype(bf16)
+
     lax.fori_loop(1, n_plane, start_note, 0)
 
-    dd = (ADAPTER_SCALE * dd * sign).astype(bf16)
-
-    def down_copy(p):
+    def start_down(k, carry):
+        p = lax.rem(me + k, n_plane)
         cols = pl.ds(pl.multiple_of(p * width, 128), width)
-        return remote(dbuf.at[:, cols], rdn.at[me], dsend.at[0], drecv.at[0], plane_dev(p))
-
-    def finish(i, carry):
-        cols = pl.ds(pl.multiple_of(i * GCOL, GCOL), GCOL)
-        dbuf[:, cols] = (nn(dd, tokens[:, cols]) * weight).astype(bf16)
-        for k in range(dests):
-            p = i * dests + k
-
-            @pl.when(p != me)
-            def _(p=p):
-                down_copy(p).start()
-
+        remote(dbuf.at[:, cols], rdn.at[me], dsend.at[0], drecv.at[0], plane_dev(p)).start()
         return carry
 
-    lax.fori_loop(0, KVH, finish, 0)
+    lax.fori_loop(1, n_plane, start_down, 0)
 
     my_cols = pl.ds(pl.multiple_of(me * width, 128), width)
 
@@ -408,28 +417,25 @@
     remote(others, others, usend.at[0], urecv.at[0], sibling).wait_recv()
     ru[me] = ubuf[:, my_cols]
 
-    def up_sum(p, acc):
-        return acc + notes[p][:, HD - 1 : HD] * ru[p].astype(f32)
-
-    acc = lax.fori_loop(0, n_plane, up_sum, jnp.zeros((RANK, width), f32))
-    zu[zi] = (ADAPTER_SCALE * acc).astype(bf16)
+    def weighted(buf):
+        acc = jnp.zeros((RANK, width), f32)
+        for p in range(n_plane):
+            w = jnp.concatenate([notes[p][1:2]] * (width // HD), axis=1)
+            acc = acc + w * buf[p].astype(f32)
+        return acc
+
+    zu[zi] = (ADAPTER_SCALE * weighted(ru)).astype(bf16)
     z_start(zu, zusend.at[0], zurecv.at[0])
-
-    def note_sum(p, acc):
-        return acc + notes[p]
-
-    znotes[zi] = lax.fori_loop(1, n_plane, note_sum, notes[0])
+    loss_sum = notes[0][0:1]
+    for p in range(1, n_plane):
+        loss_sum = loss_sum + notes[p][0:1]
+    znotes[zi] = loss_sum
     z_start(znotes, znsend.at[0], znrecv.at[0])
 
     others = rdn.at[pl.ds(0, n_plane - 1)]
     remote(others, others, dsend.at[0], drecv.at[0], sibling).wait_recv()
     rdn[me] = dbuf[:, my_cols]
-
-    def down_sum(p, acc):
-        return acc + rdn[p].astype(f32)
-
-    acc = lax.fori_loop(0, n_plane, down_sum, jnp.zeros((RANK, width), f32))
-    zd[zi] = acc.astype(bf16)
+    zd[zi] = weighted(rdn).astype(bf16)
     z_start(zd, zdsend.at[0], zdrecv.at[0])
 
     grads[pl.ds(0, RANK), my_cols] = z_end(zu, zusend.at[0], zurecv.at[0]).astype(bf16)
@@ -502,10 +508,13 @@
             pltpu.VMEM((n_z, RANK, width), bf16),
             pltpu.VMEM((2, KVH, HD, 2 * LANES), bf16),
             pltpu.VMEM((prefix, HD), bf16),
+            pltpu.VMEM((2, HD, HALF), bf16),
             pltpu.VMEM((prefix, HD), f32),
             pltpu.VMEM((rows, HD), f32),
+            pltpu.VMEM((2, 2, prefix + STEP, HALF), f32),
+            pltpu.VMEM((2, 2, 1, HALF), f32),
             pltpu.VMEM((rows, GCOL), bf16),
-            pltpu.VMEM((n_plane, 1, 128), f32),
+            pltpu.VMEM((n_plane, 2, 128), f32),
             pltpu.VMEM((n_z, 1, 128), f32),
             dma((12,)),
             *[dma((3,))] * 4,

time: 66 us -> 61.1 us (0.926)
  Pallas kernels: 60.7 us -> 55.9 us
    pallas_call x1, Pallas kernels: 60.7 us -> 55.9 us  [local(): pl.pallas_call(functools.partial(kernel, (n_cont, n_z)), out_shape=(jax.S...]
where the time goes in v4:
time: 61.1 us; the launch traced here: 61 us
  Pallas kernels  55.9 us (91%)
  between operations  3.05 us (5%)
  other arithmetic  2.07 us (3%)
    pallas_call x1, Pallas kernels, local(): pl.pallas_call(functools.partial(kernel, (n_cont, n_z)), out_shape=(jax.S...  55.9 us
    convert_element_type x1, other arithmetic, local(): return (loss[0, 0], grads[RANK:].astype(f32), grads[0:RANK].astype(f32))  2.07 us

profile of v4, /device:TPU:1, one launch (start us, length us, event | category | flops | bytes accessed | tf_op | source)
XLA Modules:
  0.0 61.0 jit_solution(3131375790051682395)
XLA Ops:
  1.3 55.9 %shard_map.139 = (bf16[32,8192]{1,0:T(8,128)(2,1)}, f32[1,128]{1,0:T(1,128)}) custom-call(bf16[128,8192]{1,0:T(8,128)(2,1)} %tokens_hbm.1, bf16[128,8192]{1,0:T(8,128)(2,1)} %fq_hbm.1, bf16[128,1024]{1,0:T(8,128)(2,1)} %sk_hbm.1, bf16[128,1024]{1,0:T(8,128)(2,1)} %sv_hbm.1, bf16[32,1024]{1,0:T(8,128)(2,1)} %ks_hbm.1, bf16[32,1024]{1,0:T(8,128)(2,1)} %vs_hbm.1, ...), custom_call_target="tpu_custom_call" | custom-call | tf_op jit(solution)/shard_map/pallas_call | solution.py:481
  57.1 2.1 %slice_convert_fusion = (f32[16,8192]{1,0:T(8,128)}, f32[16,8192]{1,0:T(8,128)}) fusion(bf16[32,8192]{1,0:T(8,128)(2,1)} %get-tuple-element.6), kind=kLoop, calls=%fused_computation | loop fusion | flops 262144 | bytes 1572864 | tf_op jit(solution)/shard_map/convert_element_type | solution.py:527

commit v5 on v4

--- a/solution.py
+++ b/solution.py
@@ -49,7 +49,7 @@
     lens_hbm, plen_hbm, mask_hbm,
     grads, loss_out,
     tokens, fq, sk, sv, dmap, up, vshard, rd, lens, plen, mask,
-    kv, shard, ubuf, dbuf, ru, rdn, zu, zd, qt, seen, picks, rvf, rvs, sbuf, mbuf, gbuf, notes, znotes,
+    kv, shard, ubuf, dbuf, ru, rdn, zu, zd, qt, seen, picks, rvf, rvt, rvs, rvst, rvx, sbuf, mbuf, gbuf, notes, znotes,
     local_sem, gsend, grecv, fsend, frecv, usend, urecv, dsend, drecv, nsend, nrecv,
     zusend, zurecv, zdsend, zdrecv, znsend, znrecv, ausend, aurecv, adsend, adrecv,
     susend, surecv, sdsend, sdrecv,
@@ -123,8 +123,11 @@
 
     ld_vs.wait()
     ld_rd.wait()
-    rd2 = jnp.concatenate([rd[...], rd[...]], axis=0)
-    row_g = lax.rem(iota((HD, HD), 0), HQ) // HPG
+    rdf = rd[...].astype(f32)
+    rd2 = jnp.concatenate(
+        [rdf[(i // 2) * HPG : (i // 2 + 1) * HPG] for i in range(2 * KVH)], axis=0
+    ).astype(bf16)
+    row_g = iota((HD, HD), 0) // (2 * HPG)
 
     def rv_of(values):
         total = None
@@ -134,18 +137,21 @@
             total = part if total is None else total + part
         return total
 
-    rv = rv_of(vshard[...])
-    high = rv.astype(bf16).astype(f32)
-    shard[:, 0:HD] = jnp.where(iota(rv.shape, 1) < HQ, high, rv - high).astype(bf16)
+    def parts_of(x):
+        high = x.astype(bf16).astype(f32)
+        return jnp.where(lax.rem(iota(x.shape, 1) // HPG, 2) == 0, high, x - high).astype(bf16)
+
+    shard[:, 0:HD] = parts_of(rv_of(vshard[...]))
     ld_ks.wait()
     kv[core, chip] = shard[...]
 
     pl.semaphore_wait(barrier, n_plane - 1 + n_z - 1)
 
-    part_width = 3 * HD
+    part_at = (0, 2, 3, 6, 9)
+    n_parts = len(part_at) - 1
 
     def part_cols(n):
-        return pl.ds(pl.multiple_of(n * part_width, HD), part_width)
+        return pl.ds(part_at[n] * HD, (part_at[n + 1] - part_at[n]) * HD)
 
     def block_cols(n):
         return pl.ds(pl.multiple_of(n * HD, HD), HD)
@@ -173,6 +179,7 @@
         forward_copy(n, core).start()
 
     issue(0)
+    issue(1)
 
     ld_dmap.wait()
     ld_tokens.wait()
@@ -206,7 +213,10 @@
 
     ld_sv.wait()
     rvs[...] = rv_of(sv[...])
-    issue(1)
+    step_parts = parts_of(rvs[...]).astype(f32)
+    for c in range(2):
+        rvst[c] = step_parts[c * STEP : (c + 1) * STEP].T.astype(bf16)
+    issue(2)
     ld_fq.wait()
     ld_up.wait()
     ld_sk.wait()
@@ -225,7 +235,7 @@
         return carry
 
     lax.fori_loop(0, KVH, prepare, 0)
-    issue(2)
+    issue(3)
     for c in range(2):
         picks[c] = (iota((HD, HALF), 0) == c).astype(f32).astype(bf16)
 
@@ -233,7 +243,7 @@
         cols = pl.ds(pl.multiple_of(p * width, 128), width)
         return remote(ubuf.at[:, cols], ru.at[me], usend.at[0], urecv.at[0], plane_dev(p))
 
-    units = [(c, j) for c in range(2) for j in range(2)]
+    units = [(c, j) for j in range(2) for c in range(2)]
 
     def stage_a(g, u, slot):
         c, j = units[u]
@@ -253,27 +263,36 @@
     def expand(rows, g, j):
         parts = []
         for i in range(2):
-            index = g * HPG + 4 * j + 2 * i + iota(rows.shape, 1) // STEP
+            index = g * (2 * HPG) + 4 * j + 2 * i + iota(rows.shape, 1) // STEP
             parts.append(jnp.take_along_axis(rows, index, axis=1))
         return jnp.concatenate(parts, axis=1)
 
-    def softmax(slot, s, rv_p, rv_s):
+    def weights(slot, s):
         peak = mbuf[slot, s]
         e_p = jnp.exp2(sbuf[slot, s, pl.ds(0, prefix), :] - peak)
         e_s = jnp.exp2(sbuf[slot, s, pl.ds(prefix, STEP), :] - peak)
+        return e_p, e_s
+
+    def stage_b(g, u, slot):
+        c, j = units[u]
+        rv_p = rvx[j]
+        rv_s = expand(rvs[pl.ds(c * STEP, STEP), :], g, j)
+        e_p, e_s = weights(slot, 0)
         total = jnp.sum(e_p, axis=0, keepdims=True) + jnp.sum(e_s, axis=0, keepdims=True)
         o = jnp.sum(e_p * rv_p, axis=0, keepdims=True) + jnp.sum(e_s * rv_s, axis=0, keepdims=True)
         inverse = 1.0 / total
-        return e_p, e_s, inverse, o * inverse
-
-    def stage_b(g, u, slot):
-        c, j = units[u]
-        rv_p = expand(rvf[...], g, j)
-        rv_s = expand(rvs[pl.ds(c * STEP, STEP), :], g, j)
-        e_p, e_s, inverse, o = softmax(slot, 0, rv_p, rv_s)
+        o = o * inverse
         ds_p = (e_p * (rv_p - o)).astype(bf16)
         ds_s = (e_s * (rv_s - o)).astype(bf16)
-        o_ref = softmax(slot, 1, rv_p, rv_s)[3]
+        e_p, e_s = weights(slot, 1)
+        own = pl.ds(pl.multiple_of(g * 16, 16), 16)
+        sums = nn(jnp.concatenate([rvt[own, :], jnp.ones((16, prefix), bf16)], axis=0), e_p.astype(bf16))
+        sums = sums + nn(
+            jnp.concatenate([rvst[c, own, :], jnp.ones((16, STEP), bf16)], axis=0), e_s.astype(bf16)
+        )
+        shape = (16, HALF)
+        mine = lax.rem(iota(shape, 0), HPG) == 4 * j + iota(shape, 1) // STEP
+        o_ref = jnp.sum(jnp.where(mine, sums[0:16], 0.0), axis=0, keepdims=True) / sums[16:17]
         return ds_p, ds_s, inverse * FACTOR, o - o_ref
 
     def stage_c(g, u, kp_t, ds_p, ds_s, scale):
@@ -302,69 +321,74 @@
             def _(p=p):
                 up_copy(p).start()
 
-    def group_step(g, carry):
+    def group_body(g, carry, first):
         accs = list(carry[:4])
-
-        for n in (1, 2):
-
-            @pl.when(g == 3 * n - 3)
-            def _(n=n):
-                arrive(n)
-
-            @pl.when(g == 3 * n - 2)
-            def _(n=n):
-                forward_copy(n, 1 - core).wait_recv()
-
-        @pl.when(g >= 2)
-        def _():
-            send_up(g - 2)
-
-        dd = tail(jnp.maximum(g - 1, 0), carry[4])
+        following = jnp.minimum(g + 1, KVH - 1)
+        dd = carry[4] if first else tail(g - 1, carry[4])
         kp_t = kv[:, :, :, block_cols(g + 1)].reshape(prefix, HD).T
         for u in range(4):
+            if u == 1:
+                rvx[1] = expand(rvf[...], g, 1)
+            if u == 3:
+                rvx[0] = expand(rvf[...], following, 0)
             if u < 3:
                 stage_a(g, u + 1, (u + 1) % 2)
             else:
-                stage_a(jnp.minimum(g + 1, KVH - 1), 0, 0)
+                if first:
+                    forward_copy(1, 1 - core).wait_recv()
+                stage_a(following, 0, 0)
             ds_p, ds_s, scale, diff = stage_b(g, u, u % 2)
             accs[u] = accs[u] + diff
             stage_c(g, u, kp_t, ds_p, ds_s, scale)
         return (*accs, dd)
 
+    def group_step(g, carry):
+        @pl.when(g == 3)
+        def _():
+            arrive(3)
+
+        @pl.when(g == 4)
+        def _():
+            forward_copy(3, 1 - core).wait_recv()
+
+        @pl.when(g >= 2)
+        def _():
+            send_up(g - 2)
+
+        return group_body(g, carry, False)
+
     arrive(0)
     forward_copy(0, 1 - core).wait_recv()
-    rvx = kv[:, :, :, 0:HD].reshape(prefix, HD).astype(f32)
-    rvf[...] = rvx + pltpu.roll(rvx, HQ, 1)
+    projected = kv[:, :, :, 0:HD].reshape(prefix, HD)
+    rvt[...] = projected.T
+    projected = projected.astype(f32)
+    rvf[...] = projected + pltpu.roll(projected, HD - HPG, 1)
+    rvx[0] = expand(rvf[...], 0, 0)
 
     gbuf[...] = jnp.zeros_like(gbuf)
     stage_a(0, 0, 0)
     zero_acc = jnp.zeros((1, HALF), f32)
-    carry = lax.fori_loop(0, KVH, group_step, (zero_acc,) * 4 + (jnp.zeros((RANK, HD), f32),))
+    arrive(1)
+    carry = group_body(0, (zero_acc,) * 4 + (jnp.zeros((RANK, HD), f32),), True)
+    arrive(2)
+    forward_copy(2, 1 - core).wait_recv()
+    carry = lax.fori_loop(1, KVH, group_step, carry)
     send_up(KVH - 2)
     dd = tail(KVH - 1, carry[4])
     send_up(KVH - 1)
 
     tl = lax.rem(iota((1, HALF), 1), STEP)
-    m0 = jnp.sum(jnp.where(tl < len0, carry[0] + carry[1], 0.0), axis=1, keepdims=True)
-    m1 = jnp.sum(jnp.where(tl < len1, carry[2] + carry[3], 0.0), axis=1, keepdims=True)
+    m0 = jnp.sum(jnp.where(tl < len0, carry[0] + carry[2], 0.0), axis=1, keepdims=True)
+    m1 = jnp.sum(jnp.where(tl < len1, carry[1] + carry[3], 0.0), axis=1, keepdims=True)
     zv = BETA * (m0 - m1)
     small = jnp.exp(-jnp.abs(zv))
     loss = jnp.maximum(-zv, 0.0) + jnp.log1p(small)
     weight = (BETA * LOSS_SCALE) * jnp.where(zv >= 0.0, small, 1.0) / (1.0 + small)
 
-    notes[me] = jnp.where(iota((2, HD), 0) == 0, loss, weight)
-
-    def start_note(k, carry):
-        to = plane_dev(lax.rem(me + k, n_plane))
-        remote(notes.at[me], notes.at[me], nsend.at[0], nrecv.at[0], to).start()
-        return carry
-
     dd = (ADAPTER_SCALE * dd * sign).astype(bf16)
     for i in range(KVH):
         cols = pl.ds(i * GCOL, GCOL)
-        dbuf[:, cols] = nn(dd, tokens[:, cols]).astype(bf16)
-
-    lax.fori_loop(1, n_plane, start_note, 0)
+        dbuf[:, cols] = (nn(dd, tokens[:, cols]) * weight).astype(bf16)
 
     def start_down(k, carry):
         p = lax.rem(me + k, n_plane)
@@ -373,6 +397,15 @@
         return carry
 
     lax.fori_loop(1, n_plane, start_down, 0)
+
+    notes[me] = jnp.where(iota((2, HD), 0) == 0, loss, weight)
+
+    def start_note(k, carry):
+        to = plane_dev(lax.rem(me + k, n_plane))
+        remote(notes.at[me], notes.at[me], nsend.at[0], nrecv.at[0], to).start()
+        return carry
+
+    lax.fori_loop(1, n_plane, start_note, 0)
 
     my_cols = pl.ds(pl.multiple_of(me * width, 128), width)
 
@@ -411,45 +444,47 @@
     def all_end(row, send, to_sibling):
         remote(half_of(row, core), half_of(row, 1 - core), send, to_sibling, sibling).wait_recv()
 
+    def weighted(p):
+        return jnp.concatenate([notes[p][1:2]] * (width // HD), axis=1) * ru[p].astype(f32)
+
+    others = rdn.at[pl.ds(0, n_plane - 1)]
+    remote(others, others, dsend.at[0], drecv.at[0], sibling).wait_recv()
+    rdn[me] = dbuf[:, my_cols]
+    acc = rdn[0].astype(f32)
+    for p in range(1, n_plane):
+        acc = acc + rdn[p].astype(f32)
+    zd[zi] = acc.astype(bf16)
+    z_start(zd, zdsend.at[0], zdrecv.at[0])
+
     others = notes.at[pl.ds(0, n_plane - 1)]
     remote(others, others, nsend.at[0], nrecv.at[0], sibling).wait_recv()
     others = ru.at[pl.ds(0, n_plane - 1)]
     remote(others, others, usend.at[0], urecv.at[0], sibling).wait_recv()
     ru[me] = ubuf[:, my_cols]
-
-    def weighted(buf):
-        acc = jnp.zeros((RANK, width), f32)
-        for p in range(n_plane):
-            w = jnp.concatenate([notes[p][1:2]] * (width // HD), axis=1)
-            acc = acc + w * buf[p].astype(f32)
-        return acc
-
-    zu[zi] = (ADAPTER_SCALE * weighted(ru)).astype(bf16)
+    acc = weighted(0)
+    for p in range(1, n_plane):
+        acc = acc + weighted(p)
+    zu[zi] = (ADAPTER_SCALE * acc).astype(bf16)
     z_start(zu, zusend.at[0], zurecv.at[0])
+
     loss_sum = notes[0][0:1]
     for p in range(1, n_plane):
         loss_sum = loss_sum + notes[p][0:1]
     znotes[zi] = loss_sum
     z_start(znotes, znsend.at[0], znrecv.at[0])
 
-    others = rdn.at[pl.ds(0, n_plane - 1)]
-    remote(others, others, dsend.at[0], drecv.at[0], sibling).wait_recv()
-    rdn[me] = dbuf[:, my_cols]
-    zd[zi] = weighted(rdn).astype(bf16)
-    z_start(zd, zdsend.at[0], zdrecv.at[0])
-
+    grads[pl.ds(RANK, RANK), my_cols] = z_end(zd, zdsend.at[0], zdrecv.at[0]).astype(bf16)
+    all_start(RANK, adsend.at[0], adrecv.at[0])
     grads[pl.ds(0, RANK), my_cols] = z_end(zu, zusend.at[0], zurecv.at[0]).astype(bf16)
     all_start(0, ausend.at[0], aurecv.at[0])
     loss_out[...] = z_end(znotes, znsend.at[0], znrecv.at[0])
-    grads[pl.ds(RANK, RANK), my_cols] = z_end(zd, zdsend.at[0], zdrecv.at[0]).astype(bf16)
-    all_start(RANK, adsend.at[0], adrecv.at[0])
-
-    all_forward(0, aurecv.at[0], susend.at[0], surecv.at[0])
+
+    all_forward(RANK, adrecv.at[0], sdsend.at[0], sdrecv.at[0])
 
     def sent(ref, sem):
         remote(ref, ref, sem, sem, sibling).wait_send()
 
-    for n in range(3):
+    for n in range(n_parts):
         sent(kv.at[core, pl.ds(0, n_chip - 1), :, part_cols(n)], gsend.at[n])
         sent(kv.at[core, :, :, part_cols(n)], fsend.at[n])
     sent(ru.at[pl.ds(0, n_plane - 1)], usend.at[0])
@@ -459,7 +494,7 @@
     sent(zd.at[pl.ds(0, n_z - 1)], zdsend.at[0])
     sent(znotes.at[pl.ds(0, n_z - 1)], znsend.at[0])
 
-    all_forward(RANK, adrecv.at[0], sdsend.at[0], sdrecv.at[0])
+    all_forward(0, aurecv.at[0], susend.at[0], surecv.at[0])
     for row, sem in ((0, ausend), (RANK, adsend)):
         sent(grads.at[pl.ds(row, RANK), pl.ds(0, (n_half - 1) * width)], sem.at[0])
     all_end(0, susend.at[0], surecv.at[0])
@@ -510,14 +545,17 @@
             pltpu.VMEM((prefix, HD), bf16),
             pltpu.VMEM((2, HD, HALF), bf16),
             pltpu.VMEM((prefix, HD), f32),
+            pltpu.VMEM((HD, prefix), bf16),
             pltpu.VMEM((rows, HD), f32),
+            pltpu.VMEM((2, HD, STEP), bf16),
+            pltpu.VMEM((2, prefix, HALF), f32),
             pltpu.VMEM((2, 2, prefix + STEP, HALF), f32),
             pltpu.VMEM((2, 2, 1, HALF), f32),
             pltpu.VMEM((rows, GCOL), bf16),
             pltpu.VMEM((n_plane, 2, 128), f32),
             pltpu.VMEM((n_z, 1, 128), f32),
             dma((12,)),
-            *[dma((3,))] * 4,
+            *[dma((4,))] * 4,
             *[dma((1,))] * 20,
         ],
         compiler_params=pltpu.CompilerParams(

time: 61.1 us -> 61 us (level)
  no operation moved by 1% of the time
where the time goes in v5:
time: 61 us; the launch traced here: 60.9 us
  Pallas kernels  55.8 us (91%)
  between operations  3.05 us (5%)
  other arithmetic  2.07 us (3%)
    pallas_call x1, Pallas kernels, local(): pl.pallas_call(functools.partial(kernel, (n_cont, n_z)), out_shape=(jax.S...  55.8 us
    convert_element_type x1, other arithmetic, local(): return (loss[0, 0], grads[RANK:].astype(f32), grads[0:RANK].astype(f32))  2.07 us

profile of v5, /device:TPU:1, one launch (start us, length us, event | category | flops | bytes accessed | tf_op | source)
XLA Modules:
  0.0 60.9 jit_solution(990119183104325605)
XLA Ops:
  1.3 55.8 %shard_map.139 = (bf16[32,8192]{1,0:T(8,128)(2,1)}, f32[1,128]{1,0:T(1,128)}) custom-call(bf16[128,8192]{1,0:T(8,128)(2,1)} %tokens_hbm.1, bf16[128,8192]{1,0:T(8,128)(2,1)} %fq_hbm.1, bf16[128,1024]{1,0:T(8,128)(2,1)} %sk_hbm.1, bf16[128,1024]{1,0:T(8,128)(2,1)} %sv_hbm.1, bf16[32,1024]{1,0:T(8,128)(2,1)} %ks_hbm.1, bf16[32,1024]{1,0:T(8,128)(2,1)} %vs_hbm.1, ...), custom_call_target="tpu_custom_call" | custom-call | tf_op jit(solution)/shard_map/pallas_call | solution.py:516
  57.1 2.1 %slice_convert_fusion = (f32[16,8192]{1,0:T(8,128)}, f32[16,8192]{1,0:T(8,128)}) fusion(bf16[32,8192]{1,0:T(8,128)(2,1)} %get-tuple-element.6), kind=kLoop, calls=%fused_computation | loop fusion | flops 262144 | bytes 1572864 | tf_op jit(solution)/shard_map/convert_element_type | solution.py:565

commit v6 on v5

--- a/solution.py
+++ b/solution.py
@@ -18,6 +18,7 @@
 GCOL = HPG * HD
 LANES = HPG * STEP
 HALF = LANES // 2
+MASK = 16
 
 NEG = -1e30
 BETA = 0.1
@@ -49,10 +50,10 @@
     lens_hbm, plen_hbm, mask_hbm,
     grads, loss_out,
     tokens, fq, sk, sv, dmap, up, vshard, rd, lens, plen, mask,
-    kv, shard, ubuf, dbuf, ru, rdn, zu, zd, qt, seen, picks, rvf, rvt, rvs, rvst, rvx, sbuf, mbuf, gbuf, notes, znotes,
+    kv, shard, ubuf, dbuf, ru, rdn, zu, zd, qt, seen, picks, rvf, rvt, rvs, rvst, rvx, sbuf, mbuf, gbuf, dsib, dsum, ushare, lpair, notes, znotes,
     local_sem, gsend, grecv, fsend, frecv, usend, urecv, dsend, drecv, nsend, nrecv,
     zusend, zurecv, zdsend, zdrecv, znsend, znrecv, ausend, aurecv, adsend, adrecv,
-    susend, surecv, sdsend, sdrecv,
+    susend, surecv, sdsend, sdrecv, xsend, xrecv, gvsend, gvrecv, tlsend, tlrecv,
 ):
     n_cont, n_z = dims
     n_plane = 2 * n_cont
@@ -86,18 +87,23 @@
 
     barrier = pltpu.get_barrier_semaphore()
 
-    def greet_plane(k, carry):
-        pl.semaphore_signal(
-            barrier, inc=1, device_id=plane_dev(lax.rem(me + k, n_plane)), device_id_type=MESH
-        )
+    def peer(k):
+        return plane_dev(core * n_half + lax.rem(place + k, n_half))
+
+    def greet(to):
+        pl.semaphore_signal(barrier, inc=1, device_id=to, device_id_type=MESH)
+
+    def greet_peer(k, carry):
+        greet(peer(k))
         return carry
 
     def greet_z(k, carry):
-        pl.semaphore_signal(barrier, inc=1, device_id=z_dev(lax.rem(zi + k, n_z)), device_id_type=MESH)
+        greet(z_dev(lax.rem(zi + k, n_z)))
         return carry
 
-    lax.fori_loop(1, n_plane, greet_plane, 0)
+    lax.fori_loop(1, n_half, greet_peer, 0)
     lax.fori_loop(1, n_z, greet_z, 0)
+    greet(sibling)
 
     loads = []
     for i, (src, dst) in enumerate(
@@ -145,7 +151,7 @@
     ld_ks.wait()
     kv[core, chip] = shard[...]
 
-    pl.semaphore_wait(barrier, n_plane - 1 + n_z - 1)
+    pl.semaphore_wait(barrier, n_half - 1 + n_z - 1 + 1)
 
     part_at = (0, 2, 3, 6, 9)
     n_parts = len(part_at) - 1
@@ -200,11 +206,12 @@
     ld_plen.wait()
     ld_mask.wait()
     limit = plen[0]
+    seen[pl.ds(prefix, STEP), :] = jnp.zeros((STEP, MASK), bf16)
     for b in range(n_cont):
         block = 2 * (b % n_chip) + b // n_chip
         inside = block * BLOCK < limit
         fill = [jnp.where((mask[c, block] > 0) & inside, 0.0, NEG) for c in range(2)]
-        col = iota((BLOCK, HD), 1)
+        col = iota((BLOCK, MASK), 1)
         seen[pl.ds(b * BLOCK, BLOCK), :] = jnp.where(
             col == 0, fill[0], jnp.where(col == 1, fill[1], 0.0)
         ).astype(bf16)
@@ -237,11 +244,7 @@
     lax.fori_loop(0, KVH, prepare, 0)
     issue(3)
     for c in range(2):
-        picks[c] = (iota((HD, HALF), 0) == c).astype(f32).astype(bf16)
-
-    def up_copy(p):
-        cols = pl.ds(pl.multiple_of(p * width, 128), width)
-        return remote(ubuf.at[:, cols], ru.at[me], usend.at[0], urecv.at[0], plane_dev(p))
+        picks[c] = (iota((MASK, HALF), 0) == c).astype(f32).astype(bf16)
 
     units = [(c, j) for j in range(2) for c in range(2)]
 
@@ -250,10 +253,12 @@
         kp = kv[:, :, :, block_cols(g + 1)].reshape(prefix, HD)
         ks = sk[pl.ds(c * STEP, STEP), block_cols(g)]
         at = c * LANES + j * HALF
+        keys = jnp.concatenate([jnp.concatenate([kp, ks], axis=0), seen[...]], axis=1)
         for s in range(2):
             q = qt[s, g, :, at : at + HALF]
-            s_p = nn(jnp.concatenate([kp, seen[...]], axis=1), jnp.concatenate([q, picks[c]], axis=0))
-            s_s = nn(ks, q) + causal
+            scores = nn(keys, jnp.concatenate([q, picks[c]], axis=0))
+            s_p = scores[0:prefix]
+            s_s = scores[prefix:] + causal
             sbuf[slot, s, pl.ds(0, prefix), :] = s_p
             sbuf[slot, s, pl.ds(prefix, STEP), :] = s_s
             mbuf[slot, s] = jnp.maximum(
@@ -316,15 +321,18 @@
     def send_up(g):
         for i in range(dests):
             p = g * dests + i
-
-            @pl.when(p != me)
-            def _(p=p):
-                up_copy(p).start()
-
-    def group_body(g, carry, first):
+            r = lax.rem(p, n_half)
+
+            @pl.when(r != place)
+            def _(p=p, r=r):
+                cols = pl.ds(pl.multiple_of(p * width, 128), width)
+                to = plane_dev(core * n_half + r)
+                remote(ubuf.at[:, cols], ru.at[p // n_half, place], usend.at[0], urecv.at[0], to).start()
+
+    def group_body(g, carry, peeled=None):
         accs = list(carry[:4])
         following = jnp.minimum(g + 1, KVH - 1)
-        dd = carry[4] if first else tail(g - 1, carry[4])
+        dd = carry[4] if peeled == 0 else tail(g - 1, carry[4])
         kp_t = kv[:, :, :, block_cols(g + 1)].reshape(prefix, HD).T
         for u in range(4):
             if u == 1:
@@ -334,8 +342,10 @@
             if u < 3:
                 stage_a(g, u + 1, (u + 1) % 2)
             else:
-                if first:
-                    forward_copy(1, 1 - core).wait_recv()
+                if peeled is not None:
+                    forward_copy(peeled + 1, 1 - core).wait_recv()
+                if peeled == 0:
+                    arrive(2)
                 stage_a(following, 0, 0)
             ds_p, ds_s, scale, diff = stage_b(g, u, u % 2)
             accs[u] = accs[u] + diff
@@ -351,11 +361,8 @@
         def _():
             forward_copy(3, 1 - core).wait_recv()
 
-        @pl.when(g >= 2)
-        def _():
-            send_up(g - 2)
-
-        return group_body(g, carry, False)
+        send_up(g - 2)
+        return group_body(g, carry)
 
     arrive(0)
     forward_copy(0, 1 - core).wait_recv()
@@ -369,10 +376,9 @@
     stage_a(0, 0, 0)
     zero_acc = jnp.zeros((1, HALF), f32)
     arrive(1)
-    carry = group_body(0, (zero_acc,) * 4 + (jnp.zeros((RANK, HD), f32),), True)
-    arrive(2)
-    forward_copy(2, 1 - core).wait_recv()
-    carry = lax.fori_loop(1, KVH, group_step, carry)
+    carry = group_body(0, (zero_acc,) * 4 + (jnp.zeros((RANK, HD), f32),), 0)
+    carry = group_body(1, carry, 1)
+    carry = lax.fori_loop(2, KVH, group_step, carry)
     send_up(KVH - 2)
     dd = tail(KVH - 1, carry[4])
     send_up(KVH - 1)
@@ -390,22 +396,34 @@
         cols = pl.ds(i * GCOL, GCOL)
         dbuf[:, cols] = (nn(dd, tokens[:, cols]) * weight).astype(bf16)
 
+    def side(which):
+        return pl.ds(pl.multiple_of(which * n_half * width, 128), n_half * width)
+
+    def cols_of(p):
+        return pl.ds(pl.multiple_of(p * width, 128), width)
+
+    swap = remote(dbuf.at[:, side(1 - core)], dsib, xsend.at[0], xrecv.at[0], sibling)
+    swap.start()
+
+    notes[place] = jnp.where(iota((2, HD), 0) == 0, loss, weight)
+
+    def start_note(k, carry):
+        remote(notes.at[place], notes.at[place], nsend.at[0], nrecv.at[0], peer(k)).start()
+        return carry
+
+    lax.fori_loop(1, n_half, start_note, 0)
+    for h in range(2):
+        ru[h, place] = ubuf[:, cols_of(h * n_half + place)]
+
+    swap.wait_recv()
+    dsum[...] = (dbuf[:, side(core)].astype(f32) + dsib[...].astype(f32)).astype(bf16)
+
     def start_down(k, carry):
-        p = lax.rem(me + k, n_plane)
-        cols = pl.ds(pl.multiple_of(p * width, 128), width)
-        remote(dbuf.at[:, cols], rdn.at[me], dsend.at[0], drecv.at[0], plane_dev(p)).start()
+        cols = cols_of(lax.rem(place + k, n_half))
+        remote(dsum.at[:, cols], rdn.at[place], dsend.at[0], drecv.at[0], peer(k)).start()
         return carry
 
-    lax.fori_loop(1, n_plane, start_down, 0)
-
-    notes[me] = jnp.where(iota((2, HD), 0) == 0, loss, weight)
-
-    def start_note(k, carry):
-        to = plane_dev(lax.rem(me + k, n_plane))
-        remote(notes.at[me], notes.at[me], nsend.at[0], nrecv.at[0], to).start()
-        return carry
-
-    lax.fori_loop(1, n_plane, start_note, 0)
+    lax.fori_loop(1, n_half, start_down, 0)
 
     my_cols = pl.ds(pl.multiple_of(me * width, 128), width)
 
@@ -425,16 +443,13 @@
         part = grads.at[pl.ds(row, RANK), my_cols]
 
         def one(k, carry):
-            to = plane_dev(core * n_half + lax.rem(place + k, n_half))
-            remote(part, part, send, recv, to).start()
+            remote(part, part, send, recv, peer(k)).start()
             return carry
 
         lax.fori_loop(1, n_half, one, 0)
 
     def half_of(row, which):
-        return grads.at[
-            pl.ds(row, RANK), pl.ds(pl.multiple_of(which * n_half * width, 128), n_half * width)
-        ]
+        return grads.at[pl.ds(row, RANK), side(which)]
 
     def all_forward(row, recv, send, to_sibling):
         others = grads.at[pl.ds(row, RANK), pl.ds(0, (n_half - 1) * width)]
@@ -444,33 +459,43 @@
     def all_end(row, send, to_sibling):
         remote(half_of(row, core), half_of(row, 1 - core), send, to_sibling, sibling).wait_recv()
 
-    def weighted(p):
-        return jnp.concatenate([notes[p][1:2]] * (width // HD), axis=1) * ru[p].astype(f32)
-
-    others = rdn.at[pl.ds(0, n_plane - 1)]
+    others = notes.at[pl.ds(0, n_half - 1)]
+    remote(others, others, nsend.at[0], nrecv.at[0], sibling).wait_recv()
+    others = ru.at[:, pl.ds(0, n_half - 1)]
+    remote(others, others, usend.at[0], urecv.at[0], sibling).wait_recv()
+
+    def share(h):
+        acc = jnp.zeros((RANK, width), f32)
+        for r in range(n_half):
+            w = jnp.concatenate([notes[r][1:2]] * (width // HD), axis=1)
+            acc = acc + w * ru[h, r].astype(f32)
+        return acc * ADAPTER_SCALE
+
+    ushare[0] = share(1 - core).astype(bf16)
+    loss_sum = notes[0][0:1]
+    for r in range(1, n_half):
+        loss_sum = loss_sum + notes[r][0:1]
+    lpair[core] = loss_sum
+    give = remote(ushare.at[0], ushare.at[1], gvsend.at[0], gvrecv.at[0], sibling)
+    give.start()
+    tell = remote(lpair.at[core], lpair.at[core], tlsend.at[0], tlrecv.at[0], sibling)
+    tell.start()
+    mine = share(core)
+
+    others = rdn.at[pl.ds(0, n_half - 1)]
     remote(others, others, dsend.at[0], drecv.at[0], sibling).wait_recv()
-    rdn[me] = dbuf[:, my_cols]
+    rdn[place] = dsum[:, cols_of(place)]
     acc = rdn[0].astype(f32)
-    for p in range(1, n_plane):
-        acc = acc + rdn[p].astype(f32)
+    for r in range(1, n_half):
+        acc = acc + rdn[r].astype(f32)
     zd[zi] = acc.astype(bf16)
     z_start(zd, zdsend.at[0], zdrecv.at[0])
 
-    others = notes.at[pl.ds(0, n_plane - 1)]
-    remote(others, others, nsend.at[0], nrecv.at[0], sibling).wait_recv()
-    others = ru.at[pl.ds(0, n_plane - 1)]
-    remote(others, others, usend.at[0], urecv.at[0], sibling).wait_recv()
-    ru[me] = ubuf[:, my_cols]
-    acc = weighted(0)
-    for p in range(1, n_plane):
-        acc = acc + weighted(p)
-    zu[zi] = (ADAPTER_SCALE * acc).astype(bf16)
+    give.wait_recv()
+    zu[zi] = (mine + ushare[1].astype(f32)).astype(bf16)
     z_start(zu, zusend.at[0], zurecv.at[0])
-
-    loss_sum = notes[0][0:1]
-    for p in range(1, n_plane):
-        loss_sum = loss_sum + notes[p][0:1]
-    znotes[zi] = loss_sum
+    tell.wait_recv()
+    znotes[zi] = lpair[0] + lpair[1]
     z_start(znotes, znsend.at[0], znrecv.at[0])
 
     grads[pl.ds(RANK, RANK), my_cols] = z_end(zd, zdsend.at[0], zdrecv.at[0]).astype(bf16)
@@ -487,9 +512,12 @@
     for n in range(n_parts):
         sent(kv.at[core, pl.ds(0, n_chip - 1), :, part_cols(n)], gsend.at[n])
         sent(kv.at[core, :, :, part_cols(n)], fsend.at[n])
-    sent(ru.at[pl.ds(0, n_plane - 1)], usend.at[0])
-    sent(rdn.at[pl.ds(0, n_plane - 1)], dsend.at[0])
-    sent(notes.at[pl.ds(0, n_plane - 1)], nsend.at[0])
+    sent(ru.at[:, pl.ds(0, n_half - 1)], usend.at[0])
+    sent(rdn.at[pl.ds(0, n_half - 1)], dsend.at[0])
+    sent(notes.at[pl.ds(0, n_half - 1)], nsend.at[0])
+    swap.wait_send()
+    give.wait_send()
+    tell.wait_send()
     sent(zu.at[pl.ds(0, n_z - 1)], zusend.at[0])
     sent(zd.at[pl.ds(0, n_z - 1)], zdsend.at[0])
     sent(znotes.at[pl.ds(0, n_z - 1)], znsend.at[0])
@@ -505,6 +533,7 @@
 
 def local(n_cont, n_z, tokens, fq, sk, sv, kshard, vshard, dmap, up, readout, lens, plen, mask):
     n_plane = 2 * n_cont
+    n_half = n_cont
     n_chip = n_cont // 2
     width = FEATURES // n_plane
     rows = tokens.shape[0]
@@ -537,13 +566,13 @@
             pltpu.VMEM((BLOCK, cols), bf16),
             pltpu.VMEM((RANK, FEATURES), bf16),
             pltpu.VMEM((RANK, FEATURES), bf16),
-            pltpu.VMEM((n_plane, RANK, width), bf16),
-            pltpu.VMEM((n_plane, RANK, width), bf16),
+            pltpu.VMEM((2, n_half, RANK, width), bf16),
+            pltpu.VMEM((n_half, RANK, width), bf16),
             pltpu.VMEM((n_z, RANK, width), bf16),
             pltpu.VMEM((n_z, RANK, width), bf16),
             pltpu.VMEM((2, KVH, HD, 2 * LANES), bf16),
-            pltpu.VMEM((prefix, HD), bf16),
-            pltpu.VMEM((2, HD, HALF), bf16),
+            pltpu.VMEM((prefix + STEP, MASK), bf16),
+            pltpu.VMEM((2, MASK, HALF), bf16),
             pltpu.VMEM((prefix, HD), f32),
             pltpu.VMEM((HD, prefix), bf16),
             pltpu.VMEM((rows, HD), f32),
@@ -552,11 +581,15 @@
             pltpu.VMEM((2, 2, prefix + STEP, HALF), f32),
             pltpu.VMEM((2, 2, 1, HALF), f32),
             pltpu.VMEM((rows, GCOL), bf16),
-            pltpu.VMEM((n_plane, 2, 128), f32),
+            pltpu.VMEM((RANK, n_half * width), bf16),
+            pltpu.VMEM((RANK, n_half * width), bf16),
+            pltpu.VMEM((2, RANK, width), bf16),
+            pltpu.VMEM((2, 1, 128), f32),
+            pltpu.VMEM((n_half, 2, 128), f32),
             pltpu.VMEM((n_z, 1, 128), f32),
             dma((12,)),
             *[dma((4,))] * 4,
-            *[dma((1,))] * 20,
+            *[dma((1,))] * 26,
         ],
         compiler_params=pltpu.CompilerParams(
             collective_id=0, has_side_effects=True, vmem_limit_bytes=60 * 1024 * 1024

time: 61 us -> 58.2 us (0.954)
  Pallas kernels: 55.8 us -> 53 us
    pallas_call x1, Pallas kernels: 55.8 us -> 53 us  [local(): pl.pallas_call(functools.partial(kernel, (n_cont, n_z)), out_shape=(jax.S...]
where the time goes in v6:
time: 58.2 us; the launch traced here: 58.1 us
  Pallas kernels  53 us (91%)
  between operations  3.05 us (5%)
  other arithmetic  2.07 us (4%)
    pallas_call x1, Pallas kernels, local(): pl.pallas_call(functools.partial(kernel, (n_cont, n_z)), out_shape=(jax.S...  53 us
    convert_element_type x1, other arithmetic, local(): return (loss[0, 0], grads[RANK:].astype(f32), grads[0:RANK].astype(f32))  2.07 us

profile of v6, /device:TPU:1, one launch (start us, length us, event | category | flops | bytes accessed | tf_op | source)
XLA Modules:
  0.0 58.1 jit_solution(10806862042058108147)
XLA Ops:
  1.3 53.0 %shard_map.139 = (bf16[32,8192]{1,0:T(8,128)(2,1)}, f32[1,128]{1,0:T(1,128)}) custom-call(bf16[128,8192]{1,0:T(8,128)(2,1)} %tokens_hbm.1, bf16[128,8192]{1,0:T(8,128)(2,1)} %fq_hbm.1, bf16[128,1024]{1,0:T(8,128)(2,1)} %sk_hbm.1, bf16[128,1024]{1,0:T(8,128)(2,1)} %sv_hbm.1, bf16[32,1024]{1,0:T(8,128)(2,1)} %ks_hbm.1, bf16[32,1024]{1,0:T(8,128)(2,1)} %vs_hbm.1, ...), custom_call_target="tpu_custom_call" | custom-call | tf_op jit(solution)/shard_map/pallas_call | solution.py:545
  54.3 2.1 %slice_convert_fusion = (f32[16,8192]{1,0:T(8,128)}, f32[16,8192]{1,0:T(8,128)}) fusion(bf16[32,8192]{1,0:T(8,128)(2,1)} %get-tuple-element.6), kind=kLoop, calls=%fused_computation | loop fusion | flops 262144 | bytes 1572864 | tf_op jit(solution)/shard_map/convert_element_type | solution.py:598

commit v7 on v6

--- a/solution.py
+++ b/solution.py
@@ -87,22 +87,33 @@
 
     barrier = pltpu.get_barrier_semaphore()
 
-    def peer(k):
-        return plane_dev(core * n_half + lax.rem(place + k, n_half))
+    n_y = n_chip // 2
+    x = 2 * lax.rem(chip, 2) + xlo
+    y = chip // 2
+
+    def hops(o):
+        return min(o[0], n_y - o[0]) + min(o[1], 4 - o[1])
+
+    plane_offsets = sorted(
+        [(oy, ox) for oy in range(n_y) for ox in range(4) if (oy, ox) != (0, 0)], key=hops, reverse=True
+    )
+    group_offsets = [o for o in plane_offsets if o[1] % 2 == 0]
+    z_offsets = sorted(range(1, n_z), key=lambda k: min(k, n_z - k), reverse=True)
+
+    def place_at(o):
+        px = lax.rem(x + o[1], 4)
+        return lax.rem(px, 2) * n_chip + lax.rem(y + o[0], n_y) * 2 + px // 2
+
+    def device_at(r):
+        return plane_dev(core * n_half + r)
 
     def greet(to):
         pl.semaphore_signal(barrier, inc=1, device_id=to, device_id_type=MESH)
 
-    def greet_peer(k, carry):
-        greet(peer(k))
-        return carry
-
-    def greet_z(k, carry):
+    for k in z_offsets:
         greet(z_dev(lax.rem(zi + k, n_z)))
-        return carry
-
-    lax.fori_loop(1, n_half, greet_peer, 0)
-    lax.fori_loop(1, n_z, greet_z, 0)
+    for o in plane_offsets:
+        greet(device_at(place_at(o)))
     greet(sibling)
 
     loads = []
@@ -163,17 +174,14 @@
         return pl.ds(pl.multiple_of(n * HD, HD), HD)
 
     def issue(n):
-        def one(k, carry):
+        for o in group_offsets:
             remote(
                 shard.at[:, part_cols(n)],
                 kv.at[core, chip, :, part_cols(n)],
                 gsend.at[n],
                 grecv.at[n],
-                {"cont": lax.rem(chip + k, n_chip) * 2 + core},
+                device_at(place_at(o)),
             ).start()
-            return carry
-
-        lax.fori_loop(1, n_chip, one, 0)
 
     def forward_copy(n, which):
         part = kv.at[core, :, :, part_cols(n)]
@@ -407,28 +415,23 @@
 
     notes[place] = jnp.where(iota((2, HD), 0) == 0, loss, weight)
 
-    def start_note(k, carry):
-        remote(notes.at[place], notes.at[place], nsend.at[0], nrecv.at[0], peer(k)).start()
-        return carry
-
-    lax.fori_loop(1, n_half, start_note, 0)
+    for o in plane_offsets:
+        to = device_at(place_at(o))
+        remote(notes.at[place], notes.at[place], nsend.at[0], nrecv.at[0], to).start()
     for h in range(2):
         ru[h, place] = ubuf[:, cols_of(h * n_half + place)]
 
     swap.wait_recv()
     dsum[...] = (dbuf[:, side(core)].astype(f32) + dsib[...].astype(f32)).astype(bf16)
 
-    def start_down(k, carry):
-        cols = cols_of(lax.rem(place + k, n_half))
-        remote(dsum.at[:, cols], rdn.at[place], dsend.at[0], drecv.at[0], peer(k)).start()
-        return carry
-
-    lax.fori_loop(1, n_half, start_down, 0)
+    for o in plane_offsets:
+        r = place_at(o)
+        remote(dsum.at[:, cols_of(r)], rdn.at[place], dsend.at[0], drecv.at[0], device_at(r)).start()
 
     my_cols = pl.ds(pl.multiple_of(me * width, 128), width)
 
     def z_start(buf, send, recv):
-        for k in range(1, n_z):
+        for k in z_offsets:
             remote(buf.at[zi], buf.at[zi], send, recv, z_dev(lax.rem(zi + k, n_z))).start()
 
     def z_end(buf, send, recv):
@@ -442,11 +445,8 @@
     def all_start(row, send, recv):
         part = grads.at[pl.ds(row, RANK), my_cols]
 
-        def one(k, carry):
-            remote(part, part, send, recv, peer(k)).start()
-            return carry
-
-        lax.fori_loop(1, n_half, one, 0)
+        for o in plane_offsets:
+            remote(part, part, send, recv, device_at(place_at(o))).start()
 
     def half_of(row, which):
         return grads.at[pl.ds(row, RANK), side(which)]

time: 58.2 us -> 57.1 us (0.981)
  Pallas kernels: 53 us -> 51.9 us
    pallas_call x1, Pallas kernels: 53 us -> 51.9 us  [local(): pl.pallas_call(functools.partial(kernel, (n_cont, n_z)), out_shape=(jax.S...]
where the time goes in v7:
time: 57.1 us; the launch traced here: 57 us
  Pallas kernels  51.9 us (91%)
  between operations  3.05 us (5%)
  other arithmetic  2.07 us (4%)
    pallas_call x1, Pallas kernels, local(): pl.pallas_call(functools.partial(kernel, (n_cont, n_z)), out_shape=(jax.S...  51.9 us
    convert_element_type x1, other arithmetic, local(): return (loss[0, 0], grads[RANK:].astype(f32), grads[0:RANK].astype(f32))  2.07 us

profile of v7, /device:TPU:1, one launch (start us, length us, event | category | flops | bytes accessed | tf_op | source)
XLA Modules:
  0.0 57.0 jit_solution(17921061138877044664)
XLA Ops:
  1.3 51.9 %shard_map.139 = (bf16[32,8192]{1,0:T(8,128)(2,1)}, f32[1,128]{1,0:T(1,128)}) custom-call(bf16[128,8192]{1,0:T(8,128)(2,1)} %tokens_hbm.1, bf16[128,8192]{1,0:T(8,128)(2,1)} %fq_hbm.1, bf16[128,1024]{1,0:T(8,128)(2,1)} %sk_hbm.1, bf16[128,1024]{1,0:T(8,128)(2,1)} %sv_hbm.1, bf16[32,1024]{1,0:T(8,128)(2,1)} %ks_hbm.1, bf16[32,1024]{1,0:T(8,128)(2,1)} %vs_hbm.1, ...), custom_call_target="tpu_custom_call" | custom-call | tf_op jit(solution)/shard_map/pallas_call | solution.py:545
  53.2 2.1 %slice_convert_fusion = (f32[16,8192]{1,0:T(8,128)}, f32[16,8192]{1,0:T(8,128)}) fusion(bf16[32,8192]{1,0:T(8,128)(2,1)} %get-tuple-element.6), kind=kLoop, calls=%fused_computation | loop fusion | flops 262144 | bytes 1572864 | tf_op jit(solution)/shard_map/convert_element_type | solution.py:598

commit v8 on v7

--- a/solution.py
+++ b/solution.py
@@ -545,7 +545,7 @@
     grads, loss = pl.pallas_call(
         functools.partial(kernel, (n_cont, n_z)),
         out_shape=(
-            jax.ShapeDtypeStruct((2 * RANK, FEATURES), bf16),
+            pltpu.VMEM((2 * RANK, FEATURES), bf16),
             jax.ShapeDtypeStruct((1, 128), f32),
         ),
         in_specs=[anyspec] * 12,

time: 57.1 us -> 55.9 us (0.979)
  other arithmetic: 2.07 us -> 1.04 us
    convert_element_type x1, other arithmetic: 2.07 us -> 1.04 us  [local(): return (loss[0, 0], grads[RANK:].astype(f32), grads[0:RANK].astype(f32))]
where the time goes in v8:
time: 55.9 us; the launch traced here: 55.7 us
  Pallas kernels  51.7 us (92%)
  between operations  3.05 us (5%)
  other arithmetic  1.04 us (2%)
    pallas_call x1, Pallas kernels, local(): pl.pallas_call(functools.partial(kernel, (n_cont, n_z)), out_shape=(pltpu...  51.7 us

profile of v8, /device:TPU:1, one launch (start us, length us, event | category | flops | bytes accessed | tf_op | source)
XLA Modules:
  0.0 55.7 jit_solution(3678490476642001106)
XLA Ops:
  1.3 51.7 %shard_map.139 = (bf16[32,8192]{1,0:T(8,128)(2,1)S(1)}, f32[1,128]{1,0:T(1,128)}) custom-call(bf16[128,8192]{1,0:T(8,128)(2,1)} %tokens_hbm.1, bf16[128,8192]{1,0:T(8,128)(2,1)} %fq_hbm.1, bf16[128,1024]{1,0:T(8,128)(2,1)} %sk_hbm.1, bf16[128,1024]{1,0:T(8,128)(2,1)} %sv_hbm.1, bf16[32,1024]{1,0:T(8,128)(2,1)} %ks_hbm.1, bf16[32,1024]{1,0:T(8,128)(2,1)} %vs_hbm.1, ...), custom_call_target="tpu_custom_call" | custom-call | tf_op jit(solution)/shard_map/pallas_call | solution.py:545
  52.9 1.0 %slice_convert_fusion = (f32[16,8192]{1,0:T(8,128)}, f32[16,8192]{1,0:T(8,128)}) fusion(bf16[32,8192]{1,0:T(8,128)(2,1)S(1)} %get-tuple-element.6), kind=kLoop, calls=%fused_computation | loop fusion | flops 262144 | bytes 1572864 | tf_op jit(solution)/shard_map/convert_element_type | solution.py:598

commit v9 on v8

--- a/solution.py
+++ b/solution.py
@@ -400,9 +400,13 @@
     weight = (BETA * LOSS_SCALE) * jnp.where(zv >= 0.0, small, 1.0) / (1.0 + small)
 
     dd = (ADAPTER_SCALE * dd * sign).astype(bf16)
-    for i in range(KVH):
-        cols = pl.ds(i * GCOL, GCOL)
-        dbuf[:, cols] = (nn(dd, tokens[:, cols]) * weight).astype(bf16)
+
+    def down_side(which):
+        for i in range(KVH // 2):
+            cols = pl.ds(pl.multiple_of(which * n_half * width + i * GCOL, 128), GCOL)
+            dbuf[:, cols] = (nn(dd, tokens[:, cols]) * weight).astype(bf16)
+
+    down_side(1 - core)
 
     def side(which):
         return pl.ds(pl.multiple_of(which * n_half * width, 128), n_half * width)
@@ -418,6 +422,7 @@
     for o in plane_offsets:
         to = device_at(place_at(o))
         remote(notes.at[place], notes.at[place], nsend.at[0], nrecv.at[0], to).start()
+    down_side(core)
     for h in range(2):
         ru[h, place] = ubuf[:, cols_of(h * n_half + place)]
 

time: 55.9 us -> 55.8 us (level)
  no operation moved by 1% of the time
where the time goes in v9:
time: 55.8 us; the launch traced here: 55.7 us
  Pallas kernels  51.6 us (92%)
  between operations  3.05 us (5%)
  other arithmetic  1.04 us (2%)
    pallas_call x1, Pallas kernels, local(): pl.pallas_call(functools.partial(kernel, (n_cont, n_z)), out_shape=(pltpu...  51.6 us

profile of v9, /device:TPU:1, one launch (start us, length us, event | category | flops | bytes accessed | tf_op | source)
XLA Modules:
  0.0 55.7 jit_solution(14980517849317772757)
XLA Ops:
  1.3 51.6 %shard_map.139 = (bf16[32,8192]{1,0:T(8,128)(2,1)S(1)}, f32[1,128]{1,0:T(1,128)}) custom-call(bf16[128,8192]{1,0:T(8,128)(2,1)} %tokens_hbm.1, bf16[128,8192]{1,0:T(8,128)(2,1)} %fq_hbm.1, bf16[128,1024]{1,0:T(8,128)(2,1)} %sk_hbm.1, bf16[128,1024]{1,0:T(8,128)(2,1)} %sv_hbm.1, bf16[32,1024]{1,0:T(8,128)(2,1)} %ks_hbm.1, bf16[32,1024]{1,0:T(8,128)(2,1)} %vs_hbm.1, ...), custom_call_target="tpu_custom_call" | custom-call | tf_op jit(solution)/shard_map/pallas_call | solution.py:550
  52.9 1.0 %slice_convert_fusion = (f32[16,8192]{1,0:T(8,128)}, f32[16,8192]{1,0:T(8,128)}) fusion(bf16[32,8192]{1,0:T(8,128)(2,1)S(1)} %get-tuple-element.6), kind=kLoop, calls=%fused_computation | loop fusion | flops 262144 | bytes 1572864 | tf_op jit(solution)/shard_map/convert_element_type | solution.py:603

commit v10 on v9

--- a/solution.py
+++ b/solution.py
@@ -451,18 +451,27 @@
         part = grads.at[pl.ds(row, RANK), my_cols]
 
         for o in plane_offsets:
-            remote(part, part, send, recv, device_at(place_at(o))).start()
-
-    def half_of(row, which):
-        return grads.at[pl.ds(row, RANK), side(which)]
+            remote(part, part, send.at[o[1] % 2], recv.at[o[1] % 2], device_at(place_at(o))).start()
+
+    def quarter(row, which, low):
+        first = pl.multiple_of((which * n_half + low * n_chip) * width, 128)
+        return grads.at[pl.ds(row, RANK), pl.ds(first, n_chip * width)]
+
+    def pieces(row, even):
+        return grads.at[pl.ds(row, RANK), pl.ds(0, (n_chip - 1 if even else n_chip) * width)]
 
     def all_forward(row, recv, send, to_sibling):
-        others = grads.at[pl.ds(row, RANK), pl.ds(0, (n_half - 1) * width)]
-        remote(others, others, send, recv, sibling).wait_recv()
-        remote(half_of(row, core), half_of(row, core), send, to_sibling, sibling).start()
+        for way in (0, 1):
+            low = lax.rem(xlo + way, 2)
+            others = pieces(row, way == 0)
+            remote(others, others, recv.at[way], recv.at[way], sibling).wait_recv()
+            part = quarter(row, core, low)
+            remote(part, part, send.at[way], to_sibling.at[way], sibling).start()
 
     def all_end(row, send, to_sibling):
-        remote(half_of(row, core), half_of(row, 1 - core), send, to_sibling, sibling).wait_recv()
+        for way in (0, 1):
+            part = quarter(row, 1 - core, lax.rem(xlo + way, 2))
+            remote(part, part, send.at[way], to_sibling.at[way], sibling).wait_recv()
 
     others = notes.at[pl.ds(0, n_half - 1)]
     remote(others, others, nsend.at[0], nrecv.at[0], sibling).wait_recv()
@@ -504,12 +513,12 @@
     z_start(znotes, znsend.at[0], znrecv.at[0])
 
     grads[pl.ds(RANK, RANK), my_cols] = z_end(zd, zdsend.at[0], zdrecv.at[0]).astype(bf16)
-    all_start(RANK, adsend.at[0], adrecv.at[0])
+    all_start(RANK, adsend, adrecv)
     grads[pl.ds(0, RANK), my_cols] = z_end(zu, zusend.at[0], zurecv.at[0]).astype(bf16)
-    all_start(0, ausend.at[0], aurecv.at[0])
+    all_start(0, ausend, aurecv)
     loss_out[...] = z_end(znotes, znsend.at[0], znrecv.at[0])
 
-    all_forward(RANK, adrecv.at[0], sdsend.at[0], sdrecv.at[0])
+    all_forward(RANK, adrecv, sdsend, sdrecv)
 
     def sent(ref, sem):
         remote(ref, ref, sem, sem, sibling).wait_send()
@@ -527,13 +536,15 @@
     sent(zd.at[pl.ds(0, n_z - 1)], zdsend.at[0])
     sent(znotes.at[pl.ds(0, n_z - 1)], znsend.at[0])
 
-    all_forward(0, aurecv.at[0], susend.at[0], surecv.at[0])
+    all_forward(0, aurecv, susend, surecv)
     for row, sem in ((0, ausend), (RANK, adsend)):
-        sent(grads.at[pl.ds(row, RANK), pl.ds(0, (n_half - 1) * width)], sem.at[0])
-    all_end(0, susend.at[0], surecv.at[0])
-    all_end(RANK, sdsend.at[0], sdrecv.at[0])
-    sent(half_of(0, core), susend.at[0])
-    sent(half_of(RANK, core), sdsend.at[0])
+        for way in (0, 1):
+            sent(pieces(row, way == 0), sem.at[way])
+    all_end(0, susend, surecv)
+    all_end(RANK, sdsend, sdrecv)
+    for row, sem in ((0, susend), (RANK, sdsend)):
+        for way in (0, 1):
+            sent(quarter(row, core, lax.rem(xlo + way, 2)), sem.at[way])
 
 
 def local(n_cont, n_z, tokens, fq, sk, sv, kshard, vshard, dmap, up, readout, lens, plen, mask):
@@ -594,7 +605,9 @@
             pltpu.VMEM((n_z, 1, 128), f32),
             dma((12,)),
             *[dma((4,))] * 4,
-            *[dma((1,))] * 26,
+            *[dma((1,))] * 12,
+            *[dma((2,))] * 8,
+            *[dma((1,))] * 6,
         ],
         compiler_params=pltpu.CompilerParams(
             collective_id=0, has_side_effects=True, vmem_limit_bytes=60 * 1024 * 1024

time: 55.8 us -> 55.8 us (level)
  no operation moved by 1% of the time
where the time goes in v10:
time: 55.8 us; the launch traced here: 55.7 us
  Pallas kernels  51.6 us (92%)
  between operations  3.05 us (5%)
  other arithmetic  1.04 us (2%)
    pallas_call x1, Pallas kernels, local(): pl.pallas_call(functools.partial(kernel, (n_cont, n_z)), out_shape=(pltpu...  51.6 us

profile of v10, /device:TPU:1, one launch (start us, length us, event | category | flops | bytes accessed | tf_op | source)
XLA Modules:
  0.0 55.7 jit_solution(18401817116669891119)
XLA Ops:
  1.3 51.6 %shard_map.139 = (bf16[32,8192]{1,0:T(8,128)(2,1)S(1)}, f32[1,128]{1,0:T(1,128)}) custom-call(bf16[128,8192]{1,0:T(8,128)(2,1)} %tokens_hbm.1, bf16[128,8192]{1,0:T(8,128)(2,1)} %fq_hbm.1, bf16[128,1024]{1,0:T(8,128)(2,1)} %sk_hbm.1, bf16[128,1024]{1,0:T(8,128)(2,1)} %sv_hbm.1, bf16[32,1024]{1,0:T(8,128)(2,1)} %ks_hbm.1, bf16[32,1024]{1,0:T(8,128)(2,1)} %vs_hbm.1, ...), custom_call_target="tpu_custom_call" | custom-call | tf_op jit(solution)/shard_map/pallas_call | solution.py:561
  52.9 1.0 %slice_convert_fusion = (f32[16,8192]{1,0:T(8,128)}, f32[16,8192]{1,0:T(8,128)}) fusion(bf16[32,8192]{1,0:T(8,128)(2,1)S(1)} %get-tuple-element.6), kind=kLoop, calls=%fused_computation | loop fusion | flops 262144 | bytes 1572864 | tf_op jit(solution)/shard_map/convert_element_type | solution.py:616
